TPU v7x, 128 devices: a whole 4x4x4 slice. The times are simulated.
128 devices in a mesh: freq: 16 (over z, y_hi, core), blk: 8 (over y_lo, x).
Axes of the slice: x: 4, y: 4 (y_hi: 2, y_lo: 2; y = y_hi * 2 + y_lo), z: 4, core: 2. Of those that a mesh axis runs over, the one named last changes fastest.
Arguments:
- voltages: bfloat16 [2, 2048, 126976], P(None, ('freq', 'blk')), may hold values from -6 to 6
- pfb_taps: float32 [16, 4096], replicated, may hold values from -1.5 to 1.5
- order_table: int32 [8, 256], P('blk'), may hold values from 0 to 255, as said below
- lag_table: int32 [4], replicated, may hold values from 0 to 3, each once
Outputs:
- visibility: bfloat16 [128, 8, 4, 2, 256, 256], P('freq', 'blk')
- far_visibility: bfloat16 [64, 8, 2, 256, 256], P('freq', 'blk')
Inputs may be any that keep to these rules, and one draw needn't show every extreme that they name: Each row of order_table holds every number below 256 once. lag_table holds every number below 4 once.
All inputs are finite; a program needn't handle non-finite values.
Results may differ from a plain program's by a relative error of at most 0.007.
Values may be sent and summed in bfloat16 or wider, within the bound.
A program may use at most 192 MiB of HBM per device.

v0:
```python
import math

import jax
import jax.numpy as jnp
from jax import lax
from jax.sharding import PartitionSpec as P

NOUT = 128


def shifted(value, axis, steps):
    count = lax.axis_size(axis)
    pairs = [(source, (source + steps) % count) for source in range(count)]
    return lax.ppermute(value, axis, pairs)


def fourier_tables(length):
    steps_row = jnp.arange(length, dtype=jnp.int32)
    phases = steps_row[:, None] * steps_row[None, :] % length
    angles = phases.astype(jnp.float32) * (-2.0 * math.pi / length)
    return (jnp.cos(angles), jnp.sin(angles))


def filter_bank(voltages, pfb_taps, out_count):
    inputs = voltages.shape[1]
    tap_count, channels = pfb_taps.shape
    frames = voltages.shape[2] // channels
    spec_count = frames - tap_count + 1
    framed = voltages.reshape(2, inputs, frames, channels)
    filtered = jnp.zeros((2, inputs, spec_count, channels), jnp.float32)
    for tap_index in range(tap_count):
        filtered = filtered + pfb_taps[tap_index] * framed[
            :, :, tap_index : tap_index + spec_count
        ].astype(jnp.float32)
    rounded = lax.optimization_barrier(filtered.astype(jnp.bfloat16)).astype(jnp.float32)
    radix_one = 1 << (channels.bit_length() - 1) // 2
    radix_two = channels // radix_one
    real_part = rounded[0].reshape(inputs, spec_count, radix_one, radix_two)
    imag_part = rounded[1].reshape(inputs, spec_count, radix_one, radix_two)
    accuracy = lax.Precision.HIGH
    one_cos, one_sin = fourier_tables(radix_one)
    section_real = jnp.einsum("km,ismn->iskn", one_cos, real_part, precision=accuracy) - jnp.einsum(
        "km,ismn->iskn", one_sin, imag_part, precision=accuracy
    )
    section_imag = jnp.einsum("km,ismn->iskn", one_cos, imag_part, precision=accuracy) + jnp.einsum(
        "km,ismn->iskn", one_sin, real_part, precision=accuracy
    )
    rows_one = jnp.arange(radix_one, dtype=jnp.int32)
    rows_two = jnp.arange(radix_two, dtype=jnp.int32)
    angles = (rows_one[:, None] * rows_two[None, :] % channels).astype(jnp.float32) * (
        -2.0 * math.pi / channels
    )
    turn_cos = jnp.cos(angles)
    turn_sin = jnp.sin(angles)
    turned_real = section_real * turn_cos - section_imag * turn_sin
    turned_imag = section_real * turn_sin + section_imag * turn_cos
    two_cos, two_sin = fourier_tables(radix_two)
    final_real = jnp.einsum("iskn,nq->iqks", turned_real, two_cos, precision=accuracy) - jnp.einsum(
        "iskn,nq->iqks", turned_imag, two_sin, precision=accuracy
    )
    final_imag = jnp.einsum("iskn,nq->iqks", turned_real, two_sin, precision=accuracy) + jnp.einsum(
        "iskn,nq->iqks", turned_imag, two_cos, precision=accuracy
    )
    spectra = jnp.stack([final_real, final_imag]) * (1.0 / math.sqrt(channels))
    return spectra.reshape(2, inputs, out_count, -1).astype(jnp.bfloat16)


def correlate(left_side, right_side):
    depth_len = right_side.shape[-1]
    product = jnp.einsum(
        "eprok,pcok->oerc", left_side, right_side, preferred_element_type=jnp.float32
    )
    return (product * (1.0 / depth_len)).astype(jnp.bfloat16)


def take_parity(array, parity, axis):
    shape = array.shape
    split = shape[:axis] + (shape[axis] // 2, 2) + shape[axis + 1 :]
    return lax.dynamic_index_in_dim(array.reshape(split), parity, axis + 1, keepdims=False)


def place(vis_store, tile_out, lag_value, lag_table):
    slot_ids = jnp.arange(lag_table.shape[0], dtype=jnp.int32)
    slot_index = jnp.sum(jnp.where(lag_table == lag_value, slot_ids, 0))
    anchor = jnp.int32(0)
    return lax.dynamic_update_slice(
        vis_store, tile_out[:, None, None], (anchor, anchor, slot_index, anchor, anchor, anchor)
    )


def per_device(voltages, pfb_taps, order_table, lag_table):
    devices_freq = lax.axis_size("freq")
    block_count = lax.axis_size("blk")
    lag_count = block_count // 2
    spectra = filter_bank(voltages, pfb_taps, NOUT)
    inputs = spectra.shape[1]
    depth_len = spectra.shape[3]
    per_block = inputs // block_count
    outs_dev = NOUT // devices_freq
    pieces = spectra.reshape(
        2, per_block, block_count, devices_freq, outs_dev, depth_len
    ).transpose(0, 1, 3, 2, 4, 5)
    flat_pieces = pieces.reshape(2, per_block, devices_freq * block_count, outs_dev, depth_len)
    arrived = lax.all_to_all(flat_pieces, ("freq", "blk"), split_axis=2, concat_axis=1, tiled=True)
    own_block = arrived.reshape(2, -1, outs_dev, depth_len)
    own_block = jnp.take(own_block, order_table[0], axis=1)
    rows_dev = own_block.shape[1]
    left_side = jnp.stack([own_block, jnp.stack([own_block[1], -own_block[0]])])
    visibility = jnp.zeros((outs_dev, 1, lag_count, 2, rows_dev, rows_dev), jnp.bfloat16)
    visibility = place(visibility, correlate(left_side, own_block), 0, lag_table)
    position = lax.axis_index("blk")
    current = own_block
    for lag_step in range(1, lag_count):
        current = shifted(current, "blk", -1)
        visibility = place(visibility, correlate(left_side, current), lag_step, lag_table)
    parity = (position >= lag_count).astype(jnp.int32)
    arrived_far = shifted(current, "blk", -1)
    far_right = take_parity(arrived_far, parity, 2)
    far_left = take_parity(left_side, parity, 3)
    far_visibility = correlate(far_left, far_right)[:, None]
    return (visibility, far_visibility)


def solution(mesh):
    placed = (P(None, ("freq", "blk"), None), P(), P("blk", None), P())
    return jax.shard_map(
        per_device,
        mesh=mesh,
        in_specs=placed,
        out_specs=(P("freq", "blk", None, None, None, None), P("freq", "blk", None, None, None)),
        check_vma=False,
    )
```

profile of v0, /device:TPU:22, one launch (start us, length us, event | category | flops | bytes accessed | tf_op | source)
XLA Modules:
  0.0 713.6 jit_solution(12451976156024707333)
XLA Ops:
  0.6 2.3 fusion.126
  2.9 9.6 %reshape.134 = bf16[2,16,31,4096]{3,2,1,0:T(8,128)(2,1)} reshape(bf16[2,16,126976]{2,1,0:T(8,128)(2,1)} %param.4) | data formatting | bytes 16252928 | tf_op jit(solution)/shard_map/reshape | solution.py:29
  12.6 44.3 %add_convert_fusion = bf16[2,16,16,4096]{3,2,1,0:T(8,128)(2,1)} fusion(bf16[2,16,31,4096]{3,2,1,0:T(8,128)(2,1)} %reshape.134, f32[4096]{0:T(1024)S(1)} %bitcast.233, f32[4096]{0:T(1024)S(1)} %bitcast.234, f32[4096]{0:T(1024)S(1)} %bitcast.220, f32[4096]{0:T(1024)S(1)} %bitcast.221, f32[4096]{0:T(1024)S(1)} %bitcast.222, f32[4096]{0:T(1024)S(1)} %bitcast.223, ...), kind=kLoop, calls=%fused_computation.14 | loop fusion | flops 100663296 | bytes 71565312 | tf_op jit(solution)/shard_map/convert_element_type | solution.py:35
  56.9 4.0 fusion.125
  60.9 7.3 %reshape_squeeze.6 = bf16[16,16,64,64]{3,2,1,0:T(8,128)(2,1)} reshape(bf16[1,16,16,4096]{3,2,1,0:T(8,128)(2,1)} %get-tuple-element.18) | data formatting | bytes 4194304 | tf_op jit(solution)/shard_map/reshape;squeeze | solution.py:38
  68.2 0.0 copy-start.2
  68.2 9.0 %fusion.55 = f32[16,16,64,64]{3,2,1,0:T(8,128)} fusion(bf16[16,16,64,64]{3,2,1,0:T(8,128)(2,1)} %reshape_squeeze.6), kind=kOutput, calls=%fused_computation.62 | convolution fusion | flops 402710528 | bytes 6291456 | tf_op jit(solution)/shard_map/km,ismn->iskn/dot_general | solution.py:42
  77.2 0.0 copy-done.2
  77.2 5.7 fusion.63
  82.9 0.1 fusion.74
  83.0 5.7 reshape_squeeze.7
  88.8 8.9 %fusion.65 = f32[16,16,64,64]{3,2,1,0:T(8,128)} fusion(bf16[16,16,64,64]{3,2,1,0:T(8,128)(2,1)} %reshape_squeeze.7), kind=kOutput, calls=%fused_computation.72 | convolution fusion | flops 402710528 | bytes 6291456 | tf_op jit(solution)/shard_map/km,ismn->iskn/dot_general | solution.py:42
  97.6 20.0 %fusion.2 = (f32[16,16,64,64]{2,3,1,0:T(8,128)}, f32[16,16,64,64]{2,3,1,0:T(8,128)}) fusion(f32[64,64]{0,1:T(8,128)S(1)} %get-tuple-element.36, f32[64,64]{0,1:T(8,128)S(1)} %get-tuple-element.37, f32[16,16,64,64]{3,2,1,0:T(8,128)} %fusion.63, f32[16,16,64,64]{3,2,1,0:T(8,128)} %fusion.55, f32[16,16,64,64]{3,2,1,0:T(8,128)} %fusion.65, ...), kind=kOutput, calls=%fused_computation.9 | convolution fusion | flops 411099136 | bytes 23101440 | tf_op jit(solution)/shard_map/km,ismn->iskn/dot_general | solution.py:45
  117.6 7.4 %fusion.58 = f32[64,16,16,64]{3,0,2,1:T(8,128)S(1)} fusion(f32[16,16,64,64]{2,3,1,0:T(8,128)} %get-tuple-element.13), kind=kOutput, calls=%fused_computation.65 | convolution fusion | flops 402710528 | bytes 8388608 | tf_op jit(solution)/shard_map/iskn,nq->iqks/dot_general | solution.py:58
  125.0 0.0 copy-done
  125.0 0.0 slice-start.1
  125.0 6.6 fusion.60
  131.6 0.0 slice-done
  131.6 0.0 slice-done.1
  131.6 6.4 subtract_bitcast_fusion
  138.0 19.7 %copy.55 = f32[16,64,64,16]{3,2,1,0:T(8,128)} copy(f32[16,64,64,16]{2,1,3,0:T(8,128)} %subtract_bitcast_fusion) | data formatting | bytes 8388608 | tf_op jit(solution)/shard_map/sub | solution.py:58
  157.8 28.2 %stack.24 = f32[1,2,8,16,8,512]{5,4,3,2,1,0:T(8,128)} reshape(f32[16,64,64,16]{3,2,1,0:T(8,128)} %copy.55) | data formatting | bytes 8388608 | tf_op jit(solution)/shard_map/stack | solution.py:64
  185.9 12.8 %add_bitcast_fusion = f32[16,64,64,16]{2,1,3,0:T(8,128)} fusion(f32[64,16,16,64]{3,0,2,1:T(8,128)} %fusion.60, f32[16,16,64,64]{2,3,1,0:T(8,128)} %get-tuple-element.12), kind=kOutput, calls=%fused_computation.12 | convolution fusion | flops 403759104 | bytes 12582912 | tf_op jit(solution)/shard_map/iskn,nq->iqks/dot_general | solution.py:61
  198.8 19.7 %copy.58 = f32[16,64,64,16]{3,2,1,0:T(8,128)} copy(f32[16,64,64,16]{2,1,3,0:T(8,128)} %add_bitcast_fusion) | data formatting | bytes 8388608 | tf_op jit(solution)/shard_map/add | solution.py:61
  218.5 28.6 %stack.25 = f32[1,2,8,16,8,512]{5,4,3,2,1,0:T(8,128)} reshape(f32[16,64,64,16]{3,2,1,0:T(8,128)} %copy.58) | data formatting | bytes 8388608 | tf_op jit(solution)/shard_map/stack | solution.py:64
  247.1 4.1 fusion.4
  251.2 0.6 copy.59
  251.8 0.0 copy-start.8
  251.8 2.7 copy.60
  254.5 10.7 %all-to-all-start = ((bf16[2,2,128,8,512]{4,3,1,0,2:T(8,128)(2,1)}), bf16[2,2,128,8,512]{4,3,1,0,2:T(8,128)(2,1)}, u32[]{:S(2)}, u32[]{:S(2)}) async-start(bf16[2,2,128,8,512]{4,3,1,0,2:T(8,128)(2,1)} %copy.60), calls=%async_computation | async-start | bytes 8388608 | tf_op jit(solution)/shard_map/all_to_all | solution.py:104
  265.3 0.0 copy-done.8
  265.3 50.0 %all-to-all-done = bf16[2,2,128,8,512]{4,3,1,0,2:T(8,128)(2,1)} async-done(((bf16[2,2,128,8,512]{4,3,1,0,2:T(8,128)(2,1)}), bf16[2,2,128,8,512]{4,3,1,0,2:T(8,128)(2,1)}, u32[]{:S(2)}, u32[]{:S(2)}) %all-to-all-start) | async-done | bytes 4194336 | tf_op jit(solution)/shard_map/all_to_all | solution.py:104
  315.3 4.7 copy.61
  320.0 5.0 gather_fusion
  325.0 7.0 bitcast_select_fusion.1
  332.0 0.0 copy-start.3
  332.0 2.0 copy-done.3
  334.0 0.4 collective-permute-start
  334.5 94.3 %collective-permute-done = bf16[2,256,8,512]{3,1,0,2:T(8,128)(2,1)S(1)} collective-permute-done((bf16[2,256,8,512]{3,1,0,2:T(8,128)(2,1)S(1)}, bf16[2,256,8,512]{3,1,0,2:T(8,128)(2,1)S(1)}, u32[]{:S(2)}, u32[]{:S(2)}) %collective-permute-start) | collective-permute-done | bytes 4194336 | tf_op jit(solution)/shard_map/ppermute | solution.py:14
  428.8 0.0 collective-permute-start.1
  428.8 94.0 %collective-permute-done.1 = bf16[2,256,8,512]{3,1,0,2:T(8,128)(2,1)} collective-permute-done((bf16[2,256,8,512]{3,1,0,2:T(8,128)(2,1)S(1)}, bf16[2,256,8,512]{3,1,0,2:T(8,128)(2,1)}, u32[]{:S(2)}, u32[]{:S(2)}) %collective-permute-start.1) | collective-permute-done | bytes 4194336 | tf_op jit(solution)/shard_map/ppermute | solution.py:14
  522.8 0.2 collective-permute-start.2
  523.0 0.7 fusion.98
  523.8 0.0 copy-done.10
  531.2 0.0 copy-start.4
  531.3 4.7 copy.62
  535.9 0.3 fusion.124
  536.2 0.0 copy-start.1
  536.2 4.1 pad_maximum_fusion.1
  540.3 2.4 broadcast_select_fusion
  542.8 0.0 copy-done.1
  542.8 6.8 fusion.13
  549.6 66.7 %collective-permute-done.2 = bf16[2,256,8,512]{3,1,0,2:T(8,128)(2,1)} collective-permute-done((bf16[2,256,8,512]{3,1,0,2:T(8,128)(2,1)}, bf16[2,256,8,512]{3,1,0,2:T(8,128)(2,1)}, u32[]{:S(2)}, u32[]{:S(2)}) %collective-permute-start.2) | collective-permute-done | bytes 4194336 | tf_op jit(solution)/shard_map/ppermute | solution.py:14
  616.3 0.2 collective-permute-start.3
  616.5 1.0 broadcast_in_dim.51
  617.5 5.8 bitcast_dynamic-update-slice_fusion.3
  623.4 0.0 copy-start.7
  623.4 7.2 %bitcast_dynamic-update-slice_fusion.2 = bf16[8,1,4,2,256,256]{5,4,3,2,1,0:T(8,128)(2,1)S(1)} fusion(bf16[8,1,4,2,256,256]{5,4,3,2,1,0:T(8,128)(2,1)S(1)} %bitcast_dynamic-update-slice_fusion.3, s32[]{:T(128)S(6)} %select_n.118, bf16[2,256,8,512]{3,1,0,2:T(8,128)(2,1)} %copy-done.10, bf16[1,2,256,8,512]{4,2,1,0,3:T(8,128)(2,1)} %get-tuple-element.15, ...), kind=kOutput, calls=%fused_computation.45 | convolution fusion | flops 2153775104 | bytes 14680068 | tf_op jit(solution)/shard_map/eprok,pcok->oerc/dot_general | solution.py:70
  630.6 5.8 bitcast_dynamic-update-slice_fusion.1
  636.4 0.0 copy-start.6
  636.5 7.2 %bitcast_dynamic-update-slice_fusion = bf16[8,1,4,2,256,256]{5,4,3,2,1,0:T(8,128)(2,1)S(1)} fusion(bf16[8,1,4,2,256,256]{5,4,3,2,1,0:T(8,128)(2,1)S(1)} %bitcast_dynamic-update-slice_fusion.1, s32[]{:T(128)S(6)} %select_n.122, bf16[2,256,8,512]{3,1,0,2:T(8,128)(2,1)} %collective-permute-done.2, bf16[1,2,256,8,512]{4,2,1,0,3:T(8,128)(2,1)} %get-tuple-element.15, ...), kind=kOutput, calls=%fused_computation.43 | convolution fusion | flops 2153775104 | bytes 14680068 | tf_op jit(solution)/shard_map/eprok,pcok->oerc/dot_general | solution.py:70
  643.6 0.0 copy-start.5
  643.6 65.3 %collective-permute-done.3 = bf16[2,256,8,512]{3,1,0,2:T(8,128)(2,1)} collective-permute-done((bf16[2,256,8,512]{3,1,0,2:T(8,128)(2,1)}, bf16[2,256,8,512]{3,1,0,2:T(8,128)(2,1)}, u32[]{:S(2)}, u32[]{:S(2)}) %collective-permute-start.3) | collective-permute-done | bytes 4194336 | tf_op jit(solution)/shard_map/ppermute | solution.py:14
  708.9 4.5 fusion.44
  (13 shorter events, 0.0 us)
Async XLA Ops:
  68.2 9.0 %copy-start.2 = (bf16[16,16,64,64]{3,2,1,0:T(8,128)(2,1)S(1)}, bf16[16,16,64,64]{3,2,1,0:T(8,128)(2,1)}, u32[]{:S(2)}) copy-start(bf16[16,16,64,64]{3,2,1,0:T(8,128)(2,1)} %reshape_squeeze.6) | copy-start | bytes 6291460
  117.6 7.4 %copy-start = (f32[16,16,64,64]{2,3,1,0:T(8,128)S(1)}, f32[16,16,64,64]{2,3,1,0:T(8,128)}, u32[]{:S(2)}) copy-start(f32[16,16,64,64]{2,3,1,0:T(8,128)} %get-tuple-element.13) | copy-start | bytes 12582916
  117.6 14.0 %slice-start = ((s8[8388608]{0:T(1024)(128)(4,1)}), s8[4194304]{0:T(1024)(128)(4,1)S(1)}, s32[]{:S(2)}) async-start(s8[8388608]{0:T(1024)(128)(4,1)} %bitcast.213), calls=%async_computation.1 | async-start | bytes 8388608
  125.0 6.6 slice-start.1
  251.8 13.4 %copy-start.8 = (s32[1,256]{1,0:T(1,128)S(1)}, s32[1,256]{1,0:T(1,128)}, u32[]{:S(2)}) copy-start(s32[1,256]{1,0:T(1,128)} %param.6) | copy-start | bytes 3076
  254.5 60.8 %all-to-all-start = ((bf16[2,2,128,8,512]{4,3,1,0,2:T(8,128)(2,1)}), bf16[2,2,128,8,512]{4,3,1,0,2:T(8,128)(2,1)}, u32[]{:S(2)}, u32[]{:S(2)}) async-start(bf16[2,2,128,8,512]{4,3,1,0,2:T(8,128)(2,1)} %copy.60), calls=%async_computation | async-start | bytes 8388608 | tf_op jit(solution)/shard_map/all_to_all | solution.py:104
  320.0 203.0 %copy-start.9 = (s32[4]{0:T(128)S(1)}, s32[4]{0:T(128)}, u32[]{:S(2)}) copy-start(s32[4]{0:T(128)} %param.7) | copy-start | bytes 52
  332.0 2.0 copy-start.3
  334.0 94.8 %collective-permute-start = (bf16[2,256,8,512]{3,1,0,2:T(8,128)(2,1)S(1)}, bf16[2,256,8,512]{3,1,0,2:T(8,128)(2,1)S(1)}, u32[]{:S(2)}, u32[]{:S(2)}) collective-permute-start(bf16[2,256,8,512]{3,1,0,2:T(8,128)(2,1)S(1)} %bitcast_select_fusion.1), channel_id=1, source_target_pairs={{0,7},{1,0},{2,1},{3,2},{4,3},{5,4},{6,5},{7,6},{8,15},{9,8},{10,9... | collective-permute-start | bytes 12582920 | tf_op jit(solution)/shard_map/ppermute | solution.py:14
  428.8 95.0 %copy-start.10 = (bf16[2,256,8,512]{3,1,0,2:T(8,128)(2,1)}, bf16[2,256,8,512]{3,1,0,2:T(8,128)(2,1)S(1)}, u32[]{:S(2)}) copy-start(bf16[2,256,8,512]{3,1,0,2:T(8,128)(2,1)S(1)} %collective-permute-done) | copy-start | bytes 12582916
  428.8 94.0 %collective-permute-start.1 = (bf16[2,256,8,512]{3,1,0,2:T(8,128)(2,1)S(1)}, bf16[2,256,8,512]{3,1,0,2:T(8,128)(2,1)}, u32[]{:S(2)}, u32[]{:S(2)}) collective-permute-start(bf16[2,256,8,512]{3,1,0,2:T(8,128)(2,1)S(1)} %collective-permute-done), channel_id=1, source_target_pairs={{0,7},{1,0},{2,1},{3,2},{4,3},{5,4},{6,5},{7,6},{8,15},{9,8},{10,9... | collective-permute-start | bytes 12582920 | tf_op jit(solution)/shard_map/ppermute | solution.py:14
  522.8 93.5 %collective-permute-start.2 = (bf16[2,256,8,512]{3,1,0,2:T(8,128)(2,1)}, bf16[2,256,8,512]{3,1,0,2:T(8,128)(2,1)}, u32[]{:S(2)}, u32[]{:S(2)}) collective-permute-start(bf16[2,256,8,512]{3,1,0,2:T(8,128)(2,1)} %collective-permute-done.1), channel_id=1, source_target_pairs={{0,7},{1,0},{2,1},{3,2},{4,3},{5,4},{6,5},{7,6},{8,15},{9,8},{10,9... | collective-permute-start | bytes 12582920 | tf_op jit(solution)/shard_map/ppermute | solution.py:14
  531.2 4.7 copy-start.4
  536.2 6.6 copy-start.1
  616.3 92.6 %collective-permute-start.3 = (bf16[2,256,8,512]{3,1,0,2:T(8,128)(2,1)}, bf16[2,256,8,512]{3,1,0,2:T(8,128)(2,1)}, u32[]{:S(2)}, u32[]{:S(2)}) collective-permute-start(bf16[2,256,8,512]{3,1,0,2:T(8,128)(2,1)} %collective-permute-done.2), channel_id=1, source_target_pairs={{0,7},{1,0},{2,1},{3,2},{4,3},{5,4},{6,5},{7,6},{8,15},{9,8},{10,9... | collective-permute-start | bytes 12582920 | tf_op jit(solution)/shard_map/ppermute | solution.py:14
  623.4 7.2 %copy-start.7 = (bf16[1,2,256,8,512]{4,2,1,0,3:T(8,128)(2,1)S(1)}, bf16[1,2,256,8,512]{4,2,1,0,3:T(8,128)(2,1)}, u32[]{:S(2)}) copy-start(bf16[1,2,256,8,512]{4,2,1,0,3:T(8,128)(2,1)} %get-tuple-element.15) | copy-start | bytes 12582916
  636.4 72.5 %copy-start.6 = (bf16[2,256,8,512]{3,1,0,2:T(8,128)(2,1)S(1)}, bf16[2,256,8,512]{3,1,0,2:T(8,128)(2,1)}, u32[]{:S(2)}) copy-start(bf16[2,256,8,512]{3,1,0,2:T(8,128)(2,1)} %get-tuple-element.14) | copy-start | bytes 12582916
  643.6 69.8 %copy-start.5 = (bf16[8,1,4,2,256,256]{5,4,3,2,1,0:T(8,128)(2,1)}, bf16[8,1,4,2,256,256]{5,4,3,2,1,0:T(8,128)(2,1)S(1)}, u32[]{:S(2)}) copy-start(bf16[8,1,4,2,256,256]{5,4,3,2,1,0:T(8,128)(2,1)S(1)} %bitcast_dynamic-update-slice_fusion) | copy-start | bytes 25165828
where the time goes:
time: 724 us; the launch traced here: 714 us
  waiting for transfers between devices  370 us (51%)
  local copies, waits for them, and re-layouts  146 us (20%)
  matrix products  107 us (15%)
  other arithmetic  70 us (10%)
  starting transfers between devices  11.5 us (2%)
  between operations  8.62 us (1%)
    ppermute x4, waiting for transfers between devices, shifted(): return lax.ppermute(value, axis, pairs)  320 us
    another operation x2, local copies, waits for them, and re-layouts, filter_bank(): spectra = jnp.stack([final_real, final_imag]) * (1.0 / math.sqrt(channels))  56.8 us
    all_to_all x1, waiting for transfers between devices, per_device(): lax.all_to_all(flat_pieces, ('freq', 'blk'), split_axis=2, concat_axis=1,...  50 us
    convert_element_type x1, other arithmetic, filter_bank(): filtered.astype(jnp.bfloat16)  44.3 us
    dot_general x5, matrix products, correlate(): jnp.einsum('eprok,pcok->oerc', left_side, right_side, preferred_element_t...  30.5 us
    dot_general x1, matrix products, filter_bank(): jnp.einsum('km,ismn->iskn', one_cos, imag_part, precision=accuracy)  20 us
    sub x1, local copies, waits for them, and re-layouts, filter_bank(): jnp.einsum('iskn,nq->iqks', turned_real, two_cos, precision=accuracy)  19.7 us
    add x1, local copies, waits for them, and re-layouts, filter_bank(): jnp.einsum('iskn,nq->iqks', turned_real, two_sin, precision=accuracy)  19.7 us
  transfers between devices with their start and end apart: 5, of which 5 were waited for; matrix products, arithmetic and copies ran while one was open for 6% of the time, Pallas kernels for 0%

commit v1 on v0

v1 whole, which is shorter than its diff:
```python
import functools
import math

import jax
import jax.numpy as jnp
import numpy as np
from jax import lax
from jax.experimental import pallas as pl
from jax.experimental.pallas import tpu as pltpu
from jax.sharding import PartitionSpec as P

CH = 4096
TAPS = 16
SPECTRA = 16
COLS = 32
LANES = 128
GROUP = 4
GROUPS = 4


def complex_mul(value, turn):
    real, imag = value
    cos, sin = float(turn.real), float(turn.imag)
    if abs(sin) < 1e-12 and abs(cos - 1) < 1e-12:
        return value
    if abs(cos) < 1e-12 and abs(sin + 1) < 1e-12:
        return (imag, -real)
    if abs(cos + sin) < 1e-12:
        return ((real + imag) * cos, (imag - real) * cos)
    if abs(cos - sin) < 1e-12:
        return ((real - imag) * cos, (real + imag) * cos)
    return (real * cos - imag * sin, real * sin + imag * cos)


def fft_list(values):
    count = len(values)
    if count == 1:
        return values
    if count == 2:
        (ar, ai), (br, bi) = values
        return [(ar + br, ai + bi), (ar - br, ai - bi)]
    if count == 4:
        even = fft_list([values[0], values[2]])
        odd = fft_list([values[1], values[3]])
    else:
        even = fft_list(values[0::2])
        odd = fft_list(values[1::2])
    half = count // 2
    low, high = [], []
    for index in range(half):
        turned = complex_mul(odd[index], np.exp(-2j * np.pi * index / count))
        base = even[index]
        low.append((base[0] + turned[0], base[1] + turned[1]))
        high.append((base[0] - turned[0], base[1] - turned[1]))
    return low + high


def fft_columns(values):
    sections = []
    for low in range(8):
        parts = fft_list([values[8 * high + low] for high in range(4)])
        sections.append([complex_mul(part, np.exp(-2j * np.pi * low * index / 32)) for index, part in enumerate(parts)])
    result = [None] * 32
    for index in range(4):
        parts = fft_list([sections[low][index] for low in range(8)])
        for high in range(8):
            result[index + 4 * high] = parts[high]
    return result


def channelize_kernel(volt, taps, turn_cos, turn_sin, dft_high, dft_low, out, filt, z_real, z_imag, wide):
    group = pl.program_id(0)

    def filter_column(col, carry):
        weights = [jnp.broadcast_to(taps[pl.ds(t, 1), pl.ds(pl.multiple_of(col * LANES, LANES), LANES)], (16, LANES)) for t in range(TAPS)]
        for part in range(2):
            frames = []
            for frame in range(GROUP + TAPS - 1):
                start = pl.multiple_of((group * GROUP + frame) * CH + col * LANES, LANES)
                frames.append(volt[part, :, pl.ds(start, LANES)].astype(jnp.float32))
            for spec in range(GROUP):
                total = weights[0] * frames[spec]
                for tap in range(1, TAPS):
                    total = total + weights[tap] * frames[spec + tap]
                filt[part, spec, col] = total.astype(jnp.bfloat16)
        return carry

    lax.fori_loop(0, COLS, filter_column, 0)

    for spec in range(GROUP):
        for half in range(2):
            rows = slice(half * 8, half * 8 + 8)
            values = []
            for col in range(COLS):
                values.append(tuple(filt[part, spec, col].astype(jnp.float32)[rows] for part in range(2)))
            for index, (real, imag) in enumerate(fft_columns(values)):
                cos, sin = turn_cos[index], turn_sin[index]
                place = pl.ds(half * LANES + spec * COLS + index, 8, stride=2 * LANES)
                z_real[place, :] = real * cos - imag * sin
                z_imag[place, :] = real * sin + imag * cos

    def last_step(block, carry):
        rows = pl.ds(pl.multiple_of(block * 256, 256), 256)
        both = jnp.concatenate([z_real[rows, :], z_imag[rows, :]], axis=1)
        high = both.astype(jnp.bfloat16)
        low = (both - high.astype(jnp.float32)).astype(jnp.bfloat16)
        dims = (((1,), (1,)), ((), ()))
        total = lax.dot_general(dft_high[...], high, dims, preferred_element_type=jnp.float32)
        total = total + lax.dot_general(dft_low[...], high, dims, preferred_element_type=jnp.float32)
        total = total + lax.dot_general(dft_high[...], low, dims, preferred_element_type=jnp.float32)
        for part in range(2):
            for half in range(2):
                piece = total[part * 128:part * 128 + 128, half * 128:half * 128 + 128]
                wide[pl.ds(block * 4 + part * 2 + half, 128, stride=32), :] = piece
        return carry

    lax.fori_loop(0, 8, last_step, 0)

    def narrow(index, carry):
        rows = pl.ds(pl.multiple_of(index * 256, 256), 256)
        out[pl.ds(index * 8, 8), 0] = wide[rows, :].astype(jnp.bfloat16).reshape(8, 32, LANES)
        return carry

    lax.fori_loop(0, 16, narrow, 0)


def tables():
    rows = np.arange(COLS)[:, None] * np.arange(LANES)[None, :]
    angles = -2.0 * np.pi * rows / CH
    cos = np.repeat(np.cos(angles)[:, None, :], 8, 1) / 64
    sin = np.repeat(np.sin(angles)[:, None, :], 8, 1) / 64
    steps = np.arange(LANES)
    turn = -2.0 * np.pi * (steps[:, None] * steps[None, :] % LANES) / LANES
    dft = np.block([[np.cos(turn), -np.sin(turn)], [np.sin(turn), np.cos(turn)]]).astype(np.float32)
    high = jnp.asarray(dft).astype(jnp.bfloat16)
    low = (jnp.asarray(dft) - high.astype(jnp.float32)).astype(jnp.bfloat16)
    return jnp.asarray(cos, jnp.float32), jnp.asarray(sin, jnp.float32), high, low


def whole(shape):
    return pl.BlockSpec(shape, lambda *_: (0,) * len(shape))


def channelize(voltages, pfb_taps):
    cos, sin, high, low = tables()
    inputs = [voltages, pfb_taps, cos, sin, high, low]
    return pl.pallas_call(
        channelize_kernel,
        grid=(GROUPS,),
        out_shape=jax.ShapeDtypeStruct((128, GROUPS, 32, LANES), jnp.bfloat16),
        in_specs=[whole(value.shape) for value in inputs],
        out_specs=pl.BlockSpec((128, 1, 32, LANES), lambda group: (0, group, 0, 0)),
        scratch_shapes=[
            pltpu.VMEM((2, GROUP, COLS, 16, LANES), jnp.bfloat16),
            pltpu.VMEM((2048, LANES), jnp.float32),
            pltpu.VMEM((2048, LANES), jnp.float32),
            pltpu.VMEM((4096, LANES), jnp.float32),
        ],
        compiler_params=pltpu.CompilerParams(vmem_limit_bytes=56 * 2**20),
    )(*inputs)


def correlate_kernel(lag_table, arrived, order, spread, near, far, natural, rows_x, rows_y):
    block = pl.program_id(0)
    dims = (((1,), (1,)), ((), ()))

    @pl.when(block == 0)
    def _():
        def unshuffle(index, carry):
            source = pl.ds(pl.multiple_of(index * 8, 8), 8)
            for pair in range(2):
                lanes = jnp.concatenate([arrived[source, 2 * pair + step].reshape(256, LANES) for step in range(2)], axis=1)
                sorted_rows = jnp.dot(spread[...], lanes, preferred_element_type=jnp.float32).astype(jnp.bfloat16)
                for member in range(8):
                    for part in range(2):
                        start = member * 32 + part * 16
                        natural[member, pl.ds(pl.multiple_of(index * 16, 16), 16), part * 512 + pair * 256:part * 512 + pair * 256 + 256] = sorted_rows[start:start + 16]
            return carry

        lax.fori_loop(0, 16, unshuffle, 0)
        members = lax.broadcasted_iota(jnp.int32, (256, 256), 1)
        for member in range(8):
            chosen = (order[:, member:member + 1] == members).astype(jnp.bfloat16)
            picked = jnp.dot(chosen, natural[member], preferred_element_type=jnp.float32)
            rows_x[member] = picked.astype(jnp.bfloat16)
            rows_y[member, :, :512] = picked[:, 512:].astype(jnp.bfloat16)
            rows_y[member, :, 512:] = (-picked[:, :512]).astype(jnp.bfloat16)

    def tiles(other, store):
        right = rows_x[other]
        for part, left in enumerate((rows_x, rows_y)):
            value = lax.dot_general(left[block], right, dims, preferred_element_type=jnp.float32)
            store(part, (value * (1.0 / 512)).astype(jnp.bfloat16))

    for slot in range(4):
        def store_near(part, value, slot=slot):
            near[0, slot, part] = value

        tiles(lax.rem(block + lag_table[slot], 8), store_near)

    def store_far(part, value):
        far[0, part] = value

    tiles(lax.rem(block + 4, 8), store_far)


def spread_table():
    table = np.zeros((256, 256), np.float32)
    for source in range(8):
        for row in range(16):
            for half in range(2):
                table[row * 16 + source * 2 + half, source * 32 + row * 2 + half] = 1
    return jnp.asarray(table).astype(jnp.bfloat16)


def correlate(arrived, order, lag_table):
    inputs = [arrived, order, spread_table()]
    return pl.pallas_call(
        correlate_kernel,
        grid=(8,),
        out_shape=(
            jax.ShapeDtypeStruct((8, 4, 2, 256, 256), jnp.bfloat16),
            jax.ShapeDtypeStruct((8, 2, 256, 256), jnp.bfloat16),
        ),
        in_specs=[pl.BlockSpec(memory_space=pltpu.SMEM)] + [whole(value.shape) for value in inputs],
        out_specs=(
            pl.BlockSpec((1, 4, 2, 256, 256), lambda block: (block, 0, 0, 0, 0)),
            pl.BlockSpec((1, 2, 256, 256), lambda block: (block, 0, 0, 0)),
        ),
        scratch_shapes=[pltpu.VMEM((8, 256, 1024), jnp.bfloat16)] * 3,
        compiler_params=pltpu.CompilerParams(vmem_limit_bytes=56 * 2**20),
    )(lag_table, *inputs)


def per_device(voltages, pfb_taps, order_table, lag_table):
    orders = lax.all_gather(order_table, "blk", axis=0, tiled=True)
    pieces = channelize(voltages, pfb_taps)
    arrived = lax.all_to_all(pieces, ("freq", "blk"), 0, 0, tiled=True)
    near, far = correlate(arrived, orders.T, lag_table)
    visibility = lax.all_to_all(near, "blk", 0, 0, tiled=True)
    far_all = lax.all_to_all(far, "blk", 0, 0, tiled=True)
    parity = (lax.axis_index("blk") >= 4).astype(jnp.int32)
    far_own = lax.dynamic_index_in_dim(far_all.reshape(4, 2, 2, 256, 256), parity, 1, keepdims=False)
    return visibility[:, None], far_own[:, None]


def solution(mesh):
    placed = (P(None, ("freq", "blk"), None), P(), P("blk", None), P())
    return jax.shard_map(
        per_device,
        mesh=mesh,
        in_specs=placed,
        out_specs=(P("freq", "blk", None, None, None, None), P("freq", "blk", None, None, None)),
        check_vma=False,
    )
```

time: 724 us -> 290 us (0.40)
  the two profiles are of different devices: /device:TPU:22 before, /device:TPU:6 now
where the time goes in v1:
time: 290 us; the launch traced here: 289 us
  waiting for transfers between devices  115 us (40%)
  blocking collectives  84.9 us (29%)
  Pallas kernels  61.1 us (21%)
  starting transfers between devices  17.9 us (6%)
  local copies, waits for them, and re-layouts  9.61 us (3%)
    all_to_all x1, waiting for transfers between devices, per_device(): visibility = lax.all_to_all(near, 'blk', 0, 0, tiled=True)  115 us
    all_gather x1, blocking collectives, per_device(): orders = lax.all_gather(order_table, 'blk', axis=0, tiled=True)  55.1 us
    pallas_call x1, Pallas kernels, channelize(): pl.pallas_call(channelize_kernel, grid=(GROUPS,), out_shape=jax.ShapeDtyp...  40.2 us
    all_to_all x1, blocking collectives, per_device(): far_all = lax.all_to_all(far, 'blk', 0, 0, tiled=True)  29.8 us
    pallas_call x1, Pallas kernels, correlate(): pl.pallas_call(correlate_kernel, grid=(8,), out_shape=(jax.ShapeDtypeStru...  20.9 us
    all_to_all x1, starting transfers between devices, per_device(): arrived = lax.all_to_all(pieces, ('freq', 'blk'), 0, 0, tiled=True)  10.9 us
    unnamed x3, local copies, waits for them, and re-layouts  7.78 us
    all_to_all x1, starting transfers between devices, per_device(): visibility = lax.all_to_all(near, 'blk', 0, 0, tiled=True)  6.97 us
  transfers between devices with their start and end apart: 2, of which 1 were waited for; matrix products, arithmetic and copies ran while one was open for 1% of the time, Pallas kernels for 0%

profile of v1, /device:TPU:6, one launch (start us, length us, event | category | flops | bytes accessed | tf_op | source)
XLA Modules:
  0.0 289.5 jit_solution(9635087297471482001)
XLA Ops:
  0.6 40.2 %shard_map.95 = bf16[128,4,32,128]{3,2,1,0:T(8,128)(2,1)} custom-call(bf16[2,16,126976]{2,1,0:T(8,128)(2,1)} %volt.1, f32[16,4096]{1,0:T(8,128)} %taps.1, f32[32,8,128]{2,1,0:T(8,128)} %constant.21.clone.turn_cos, f32[32,8,128]{2,1,0:T(8,128)} %constant.22.clone.turn_sin, bf16[256,256]{1,0:T(8,128)(2,1)} %constant.26.dft_high, bf16[256,256]{1,0:T(8,128)(2,1)} %constant.29.dft_low), custom_call_target="tpu_custom_call" | custom-call | tf_op jit(solution)/shard_map/pallas_call | solution.py:147
  40.8 0.0 copy-start
  40.8 10.9 %all-to-all-start = ((bf16[128,4,32,128]{3,2,1,0:T(8,128)(2,1)}), bf16[128,4,32,128]{3,2,1,0:T(8,128)(2,1)}, u32[]{:S(2)}, u32[]{:S(2)}) async-start(bf16[128,4,32,128]{3,2,1,0:T(8,128)(2,1)} %shard_map.95), calls=%async_computation | async-start | bytes 8388608 | tf_op jit(solution)/shard_map/all_to_all | solution.py:238
  51.8 0.0 copy-done
  51.8 55.1 %all-gather = s32[8,1,256]{2,1,0:T(1,128)S(1)} all-gather(s32[1,1,256]{2,1,0:T(1,128)S(1)} %bitcast.10), channel_id=1, replica_groups=mesh['freq'=16,'blk'=8] {'blk'}, dimensions={0}, use_global_device_ids=true | all-gather | bytes 9216 | tf_op jit(solution)/shard_map/all_gather | solution.py:236
  106.9 0.8 copy.13
  107.7 0.0 all-to-all-done.arrived
  107.7 20.9 %shard_map.96 = (bf16[8,4,2,256,256]{4,3,2,1,0:T(8,128)(2,1)}, bf16[8,2,256,256]{3,2,1,0:T(8,128)(2,1)}) custom-call(s32[4]{0:T(128)} %lag_table.1, bf16[128,4,32,128]{3,2,1,0:T(8,128)(2,1)} %all-to-all-done.arrived, s32[256,8]{1,0:T(8,128)} %bitcast.9, bf16[256,256]{1,0:T(8,128)(2,1)} %constant.30.spread), custom_call_target="tpu_custom_call" | custom-call | tf_op jit(solution)/shard_map/pallas_call | solution.py:218
  128.5 29.8 %all_to_all.15 = bf16[8,2,256,256]{3,2,1,0:T(8,128)(2,1)S(1)} all-to-all(bf16[8,2,256,256]{3,2,1,0:T(8,128)(2,1)} %get-tuple-element.5), channel_id=1, replica_groups=mesh['freq'=16,'blk'=8] {'blk'}, dimensions={0} | all-to-all | bytes 4194304 | tf_op jit(solution)/shard_map/all_to_all | solution.py:241
  158.3 7.0 %all-to-all-start.1 = ((bf16[8,4,2,256,256]{4,3,2,1,0:T(8,128)(2,1)}), bf16[8,4,2,256,256]{4,3,2,1,0:T(8,128)(2,1)}, u32[]{:S(2)}, u32[]{:S(2)}) async-start(bf16[8,4,2,256,256]{4,3,2,1,0:T(8,128)(2,1)} %get-tuple-element.4), calls=%async_computation.1 | async-start | bytes 16777216 | tf_op jit(solution)/shard_map/all_to_all | solution.py:240
  165.3 1.0 constant_dynamic-slice_fusion
  166.3 115.4 %all-to-all-done.1 = bf16[8,4,2,256,256]{4,3,2,1,0:T(8,128)(2,1)} async-done(((bf16[8,4,2,256,256]{4,3,2,1,0:T(8,128)(2,1)}), bf16[8,4,2,256,256]{4,3,2,1,0:T(8,128)(2,1)}, u32[]{:S(2)}, u32[]{:S(2)}) %all-to-all-start.1) | async-done | bytes 8388640 | tf_op jit(solution)/shard_map/all_to_all | solution.py:240
  281.7 7.8 %copy.16 = bf16[8,1,4,2,256,256]{5,4,3,2,1,0:T(8,128)(2,1)} copy(bf16[8,1,4,2,256,256]{5,4,3,2,1,0:T(8,128)(2,1)} %bitcast.4) | data formatting | bytes 16777216
Async XLA Ops:
  40.8 10.9 %copy-start = (s32[1,256]{1,0:T(1,128)S(1)}, s32[1,256]{1,0:T(1,128)}, u32[]{:S(2)}) copy-start(s32[1,256]{1,0:T(1,128)} %param.10) | copy-start | bytes 3076
  40.8 66.8 %all-to-all-start = ((bf16[128,4,32,128]{3,2,1,0:T(8,128)(2,1)}), bf16[128,4,32,128]{3,2,1,0:T(8,128)(2,1)}, u32[]{:S(2)}, u32[]{:S(2)}) async-start(bf16[128,4,32,128]{3,2,1,0:T(8,128)(2,1)} %shard_map.95), calls=%async_computation | async-start | bytes 8388608 | tf_op jit(solution)/shard_map/all_to_all | solution.py:238
  158.3 123.4 %all-to-all-start.1 = ((bf16[8,4,2,256,256]{4,3,2,1,0:T(8,128)(2,1)}), bf16[8,4,2,256,256]{4,3,2,1,0:T(8,128)(2,1)}, u32[]{:S(2)}, u32[]{:S(2)}) async-start(bf16[8,4,2,256,256]{4,3,2,1,0:T(8,128)(2,1)} %get-tuple-element.4), calls=%async_computation.1 | async-start | bytes 16777216 | tf_op jit(solution)/shard_map/all_to_all | solution.py:240

commit v2 on v1

v2 whole, which is shorter than its diff:
```python
import functools
import math

import jax
import jax.numpy as jnp
import numpy as np
from jax import lax
from jax.experimental import pallas as pl
from jax.experimental.pallas import tpu as pltpu
from jax.sharding import PartitionSpec as P

CH = 4096
TAPS = 16
SPECTRA = 16
COLS = 32
LANES = 128
GROUP = 4
GROUPS = 4


def complex_mul(value, turn):
    real, imag = value
    cos, sin = float(turn.real), float(turn.imag)
    if abs(sin) < 1e-12 and abs(cos - 1) < 1e-12:
        return value
    if abs(cos) < 1e-12 and abs(sin + 1) < 1e-12:
        return (imag, -real)
    if abs(cos + sin) < 1e-12:
        return ((real + imag) * cos, (imag - real) * cos)
    if abs(cos - sin) < 1e-12:
        return ((real - imag) * cos, (real + imag) * cos)
    return (real * cos - imag * sin, real * sin + imag * cos)


def fft_list(values):
    count = len(values)
    if count == 1:
        return values
    if count == 2:
        (ar, ai), (br, bi) = values
        return [(ar + br, ai + bi), (ar - br, ai - bi)]
    if count == 4:
        even = fft_list([values[0], values[2]])
        odd = fft_list([values[1], values[3]])
    else:
        even = fft_list(values[0::2])
        odd = fft_list(values[1::2])
    half = count // 2
    low, high = [], []
    for index in range(half):
        turned = complex_mul(odd[index], np.exp(-2j * np.pi * index / count))
        base = even[index]
        low.append((base[0] + turned[0], base[1] + turned[1]))
        high.append((base[0] - turned[0], base[1] - turned[1]))
    return low + high


def fft_columns(values):
    sections = []
    for low in range(8):
        parts = fft_list([values[8 * high + low] for high in range(4)])
        sections.append([complex_mul(part, np.exp(-2j * np.pi * low * index / 32)) for index, part in enumerate(parts)])
    result = [None] * 32
    for index in range(4):
        parts = fft_list([sections[low][index] for low in range(8)])
        for high in range(8):
            result[index + 4 * high] = parts[high]
    return result


MESH = pl.DeviceIdType.MESH


def position():
    freq = lax.axis_index("freq")
    blk = lax.axis_index("blk")
    return (lax.rem(blk, 4), lax.rem(freq // 2, 2) * 2 + blk // 4, freq // 4, lax.rem(freq, 2))


def mesh_ids(col, row, layer, core):
    return (layer * 4 + (row // 2) * 2 + core, lax.rem(row, 2) * 4 + col)


def channelize_kernel(volt_far, taps, turn_cos, turn_sin, dft_high, dft_low, out, volt, filt, z_real, z_imag, wide, pieces, load_sem, send_sem, recv_sem, own_sem):
    def load(group):
        first = 0 if isinstance(group, int) and group == 0 else pl.multiple_of((group * GROUP + TAPS - 1) * CH, LANES)
        size = (GROUP + TAPS - 1) * CH if isinstance(group, int) and group == 0 else GROUP * CH
        place = (slice(None), slice(None), pl.ds(first, size))
        return pltpu.make_async_copy(volt_far.at[place], volt.at[place], load_sem.at[group])

    load(0).start()
    for later in range(1, GROUPS):
        load(jnp.int32(later)).start()

    col, row, layer, core = position()
    own_freq, own_blk = mesh_ids(col, row, layer, core)
    me = own_freq * 8 + own_blk

    def target(index):
        step = lax.rem(index * 75, 128)
        return mesh_ids(
            lax.rem(col + lax.rem(step, 4), 4),
            lax.rem(row + lax.rem(step // 4, 4), 4),
            lax.rem(layer + lax.rem(step // 16, 4), 4),
            lax.rem(core + step // 64, 2),
        )

    barrier = pltpu.get_barrier_semaphore()

    def greet(index, carry):
        pl.semaphore_signal(barrier, inc=1, device_id=target(index), device_id_type=MESH)
        return carry

    lax.fori_loop(1, 128, greet, 0)

    def group_step(group, carry):
        @pl.when(group == 0)
        def _():
            load(0).wait()

        @pl.when(group > 0)
        def _():
            load(group).wait()

        def filter_column(index, carry):
            weights = [jnp.broadcast_to(taps[pl.ds(t, 1), pl.ds(pl.multiple_of(index * LANES, LANES), LANES)], (16, LANES)) for t in range(TAPS)]
            for part in range(2):
                frames = []
                for frame in range(GROUP + TAPS - 1):
                    start = pl.multiple_of((group * GROUP + frame) * CH + index * LANES, LANES)
                    frames.append(volt[part, :, pl.ds(start, LANES)].astype(jnp.float32))
                for spec in range(GROUP):
                    total = weights[0] * frames[spec]
                    for tap in range(1, TAPS):
                        total = total + weights[tap] * frames[spec + tap]
                    filt[part, spec, index] = total.astype(jnp.bfloat16)
            return carry

        lax.fori_loop(0, COLS, filter_column, 0)

        for spec in range(GROUP):
            for half in range(2):
                rows = slice(half * 8, half * 8 + 8)
                values = []
                for index in range(COLS):
                    values.append(tuple(filt[part, spec, index].astype(jnp.float32)[rows] for part in range(2)))
                for index, (real, imag) in enumerate(fft_columns(values)):
                    cos, sin = turn_cos[index], turn_sin[index]
                    place = pl.ds(half * LANES + spec * COLS + index, 8, stride=2 * LANES)
                    z_real[place, :] = real * cos - imag * sin
                    z_imag[place, :] = real * sin + imag * cos

        def last_step(block, carry):
            rows = pl.ds(pl.multiple_of(block * 256, 256), 256)
            both = jnp.concatenate([z_real[rows, :], z_imag[rows, :]], axis=1)
            high = both.astype(jnp.bfloat16)
            low = (both - high.astype(jnp.float32)).astype(jnp.bfloat16)
            dims = (((1,), (1,)), ((), ()))
            total = lax.dot_general(dft_high[...], high, dims, preferred_element_type=jnp.float32)
            total = total + lax.dot_general(dft_low[...], high, dims, preferred_element_type=jnp.float32)
            total = total + lax.dot_general(dft_high[...], low, dims, preferred_element_type=jnp.float32)
            for part in range(2):
                for half in range(2):
                    piece = total[part * 128:part * 128 + 128, half * 128:half * 128 + 128]
                    wide[pl.ds(block * 4 + part * 2 + half, 128, stride=32), :] = piece
            return carry

        lax.fori_loop(0, 8, last_step, 0)

        def narrow(index, carry):
            rows = pl.ds(pl.multiple_of(index * 256, 256), 256)
            pieces[group, pl.ds(index * 8, 8)] = wide[rows, :].astype(jnp.bfloat16).reshape(8, 32, LANES)
            return carry

        lax.fori_loop(0, 16, narrow, 0)

        @pl.when(group == 0)
        def _():
            pl.semaphore_wait(barrier, 127)

        def send(index, carry):
            freq, blk = target(index)
            pltpu.make_async_remote_copy(
                src_ref=pieces.at[group, freq * 8 + blk],
                dst_ref=out.at[group, me],
                send_sem=send_sem.at[group],
                recv_sem=recv_sem.at[group],
                device_id=(freq, blk),
                device_id_type=MESH,
            ).start()
            return carry

        lax.fori_loop(1, 128, send, 0)
        pltpu.make_async_copy(pieces.at[group, me], out.at[group, me], own_sem.at[group]).start()
        return carry

    lax.fori_loop(0, GROUPS, group_step, 0)

    def finish(group, carry):
        pltpu.make_async_copy(pieces.at[group, me], out.at[group, me], own_sem.at[group]).wait()
        others = pl.ds(0, 127)
        pltpu.make_async_copy(pieces.at[group, others], out.at[group, others], send_sem.at[group]).wait()
        pltpu.make_async_copy(pieces.at[group, others], out.at[group, others], recv_sem.at[group]).wait()
        return carry

    lax.fori_loop(0, GROUPS, finish, 0)


def tables():
    rows = np.arange(COLS)[:, None] * np.arange(LANES)[None, :]
    angles = -2.0 * np.pi * rows / CH
    cos = np.repeat(np.cos(angles)[:, None, :], 8, 1) / 64
    sin = np.repeat(np.sin(angles)[:, None, :], 8, 1) / 64
    steps = np.arange(LANES)
    turn = -2.0 * np.pi * (steps[:, None] * steps[None, :] % LANES) / LANES
    dft = np.block([[np.cos(turn), -np.sin(turn)], [np.sin(turn), np.cos(turn)]]).astype(np.float32)
    high = jnp.asarray(dft).astype(jnp.bfloat16)
    low = (jnp.asarray(dft) - high.astype(jnp.float32)).astype(jnp.bfloat16)
    return jnp.asarray(cos, jnp.float32), jnp.asarray(sin, jnp.float32), high, low


def whole(shape):
    return pl.BlockSpec(shape, lambda *_: (0,) * len(shape))


def channelize(voltages, pfb_taps):
    cos, sin, high, low = tables()
    inputs = [pfb_taps, cos, sin, high, low]
    return pl.pallas_call(
        channelize_kernel,
        out_shape=jax.ShapeDtypeStruct((GROUPS, 128, 32, LANES), jnp.bfloat16),
        in_specs=[pl.BlockSpec(memory_space=pl.ANY)] + [pl.BlockSpec(memory_space=pltpu.VMEM)] * 5,
        out_specs=pl.BlockSpec(memory_space=pl.ANY),
        scratch_shapes=[
            pltpu.VMEM(voltages.shape, jnp.bfloat16),
            pltpu.VMEM((2, GROUP, COLS, 16, LANES), jnp.bfloat16),
            pltpu.VMEM((2048, LANES), jnp.float32),
            pltpu.VMEM((2048, LANES), jnp.float32),
            pltpu.VMEM((4096, LANES), jnp.float32),
            pltpu.VMEM((GROUPS, 128, 32, LANES), jnp.bfloat16),
        ] + [pltpu.SemaphoreType.DMA((GROUPS,))] * 4,
        compiler_params=pltpu.CompilerParams(vmem_limit_bytes=48 * 2**20, collective_id=0, has_side_effects=True),
        cost_estimate=pl.CostEstimate(flops=10**10, bytes_accessed=16 * 2**20, transcendentals=0),
    )(voltages, *inputs)


def correlate_kernel(lag_table, arrived, order, spread, near, far, natural, rows_x, rows_y, tiles, far_tiles, sems):
    blk = lax.axis_index("blk")
    freq = lax.axis_index("freq")
    dims = (((1,), (1,)), ((), ()))
    barrier = pltpu.get_barrier_semaphore()
    col, side = lax.rem(blk, 4), blk // 4

    def target(index):
        step = lax.rem(index * 3 + 1, 8)
        return step, lax.rem(side + step // 4, 2) * 4 + lax.rem(col + lax.rem(step, 4), 4)

    for step in range(1, 8):
        pl.semaphore_signal(barrier, inc=1, device_id=(freq, lax.rem(blk + step, 8)), device_id_type=MESH)

    def unshuffle(index, carry):
        source = pl.ds(pl.multiple_of(index * 8, 8), 8)
        for pair in range(2):
            lanes = jnp.concatenate([arrived[2 * pair + step, source].reshape(256, LANES) for step in range(2)], axis=1)
            sorted_rows = jnp.dot(spread[...], lanes, preferred_element_type=jnp.float32).astype(jnp.bfloat16)
            for member in range(8):
                for part in range(2):
                    start = member * 32 + part * 16
                    natural[member, pl.ds(pl.multiple_of(index * 16, 16), 16), part * 512 + pair * 256:part * 512 + pair * 256 + 256] = sorted_rows[start:start + 16]
        return carry

    lax.fori_loop(0, 16, unshuffle, 0)
    members = lax.broadcasted_iota(jnp.int32, (256, 256), 1)
    for member in range(8):
        chosen = (order[:, member:member + 1] == members).astype(jnp.bfloat16)
        picked = jnp.dot(chosen, natural[member], preferred_element_type=jnp.float32)
        rows_x[member] = picked.astype(jnp.bfloat16)
        rows_y[member, :, :512] = picked[:, 512:].astype(jnp.bfloat16)
        rows_y[member, :, 512:] = (-picked[:, :512]).astype(jnp.bfloat16)
    pl.semaphore_wait(barrier, 7)

    def tile(left, other, part):
        value = lax.dot_general((rows_x, rows_y)[part][left], rows_x[other], dims, preferred_element_type=jnp.float32)
        return (value * (1.0 / 512)).astype(jnp.bfloat16)

    def post(is_own, dest, source, place, send, receive, own):
        @pl.when(is_own)
        def _():
            pltpu.make_async_copy(source, place, own).start()

        @pl.when(jnp.logical_not(is_own))
        def _():
            pltpu.make_async_remote_copy(src_ref=source, dst_ref=place, send_sem=send, recv_sem=receive, device_id=(freq, dest), device_id_type=MESH).start()

    parity = lax.rem(blk, 2)

    def near_step(index, carry):
        slot, turn = index // 8, lax.rem(index, 8)
        step, dest = target(turn)
        other = lax.rem(dest + lag_table[slot], 8)
        for part in range(2):
            tiles[index, part] = tile(dest, other, part)
            post(step == 0, dest, tiles.at[index, part], near.at[blk, slot, part], sems.at[0], sems.at[1], sems.at[2])
        return carry

    lax.fori_loop(0, 32, near_step, 0)

    def far_step(index, carry):
        dest = parity * 4 + lax.rem(col + index, 4)
        for part in range(2):
            far_tiles[index, part] = tile(dest, lax.rem(dest + 4, 8), part)
            post(dest == blk, dest, far_tiles.at[index, part], far.at[blk // 2, part], sems.at[3], sems.at[4], sems.at[5])
        return carry

    lax.fori_loop(0, 4, far_step, 0)

    own_near = pltpu.make_async_copy(tiles.at[pl.ds(0, 4)], near.at[0], sems.at[2])
    own_near.wait()
    for sem in (0, 1):
        pltpu.make_async_copy(near.at[pl.ds(0, 7)], near.at[pl.ds(0, 7)], sems.at[sem]).wait()
    has_own = parity == side

    @pl.when(has_own)
    def _():
        pltpu.make_async_copy(far_tiles.at[0], far.at[0], sems.at[5]).wait()
        for sem in (3, 4):
            pltpu.make_async_copy(far_tiles.at[pl.ds(0, 3)], far.at[pl.ds(0, 3)], sems.at[sem]).wait()

    @pl.when(jnp.logical_not(has_own))
    def _():
        for sem in (3, 4):
            pltpu.make_async_copy(far_tiles, far, sems.at[sem]).wait()


def correlate(arrived, order, lag_table):
    inputs = [arrived, order, spread_table()]
    return pl.pallas_call(
        correlate_kernel,
        out_shape=(
            jax.ShapeDtypeStruct((8, 4, 2, 256, 256), jnp.bfloat16),
            jax.ShapeDtypeStruct((4, 2, 256, 256), jnp.bfloat16),
        ),
        in_specs=[pl.BlockSpec(memory_space=pltpu.SMEM)] + [pl.BlockSpec(memory_space=pltpu.VMEM)] * 3,
        out_specs=(pl.BlockSpec(memory_space=pl.ANY), pl.BlockSpec(memory_space=pl.ANY)),
        scratch_shapes=[pltpu.VMEM((8, 256, 1024), jnp.bfloat16)] * 3
        + [pltpu.VMEM((32, 2, 256, 256), jnp.bfloat16), pltpu.VMEM((4, 2, 256, 256), jnp.bfloat16), pltpu.SemaphoreType.DMA((6,))],
        compiler_params=pltpu.CompilerParams(vmem_limit_bytes=48 * 2**20, collective_id=1, has_side_effects=True),
        cost_estimate=pl.CostEstimate(flops=10**10, bytes_accessed=16 * 2**20, transcendentals=0),
    )(lag_table, *inputs)


def per_device(voltages, pfb_taps, order_table, lag_table):
    orders = lax.all_gather(order_table, "blk", axis=0, tiled=True)
    arrived = channelize(voltages, pfb_taps)
    near, far = correlate(arrived, orders.T, lag_table)
    return near[:, None], far[:, None]


def spread_table():
    table = np.zeros((256, 256), np.float32)
    for source in range(8):
        for row in range(16):
            for half in range(2):
                table[row * 16 + source * 2 + half, source * 32 + row * 2 + half] = 1
    return jnp.asarray(table).astype(jnp.bfloat16)


def solution(mesh):
    placed = (P(None, ("freq", "blk"), None), P(), P("blk", None), P())
    return jax.shard_map(
        per_device,
        mesh=mesh,
        in_specs=placed,
        out_specs=(P("freq", "blk", None, None, None, None), P("freq", "blk", None, None, None)),
        check_vma=False,
    )
```

time: 290 us -> 224 us (0.77)
  the two profiles are of different devices: /device:TPU:6 before, /device:TPU:1 now
where the time goes in v2:
time: 224 us; the launch traced here: 222 us
  Pallas kernels  192 us (86%)
  blocking collectives  16.2 us (7%)
  local copies, waits for them, and re-layouts  13.4 us (6%)
    pallas_call x1, Pallas kernels, correlate(): pl.pallas_call(correlate_kernel, out_shape=(jax.ShapeDtypeStruct((8, 4, 2...  116 us
    pallas_call x1, Pallas kernels, channelize(): pl.pallas_call(channelize_kernel, out_shape=jax.ShapeDtypeStruct((GROUPS,...  76 us
    all_gather x1, blocking collectives, per_device(): orders = lax.all_gather(order_table, 'blk', axis=0, tiled=True)  16.2 us
    unnamed x16, local copies, waits for them, and re-layouts  13.3 us

profile of v2, /device:TPU:1, one launch (start us, length us, event | category | flops | bytes accessed | tf_op | source)
XLA Modules:
  0.0 222.0 jit_solution(1621791706662981610)
XLA Ops:
  0.6 16.2 %all-gather = s32[8,1,256]{2,1,0:T(1,128)S(1)} all-gather(s32[1,1,256]{2,1,0:T(1,128)} %bitcast.13), channel_id=1, replica_groups=mesh['freq'=16,'blk'=8] {'blk'}, dimensions={0}, use_global_device_ids=true | all-gather | bytes 9216 | tf_op jit(solution)/shard_map/all_gather | solution.py:353
  16.8 0.1 copy.15
  16.9 0.0 copy-start
  17.0 0.9 copy-done
  17.9 0.0 copy-start.2
  17.9 0.9 copy-done.2
  18.8 0.0 copy-start.4
  18.8 0.9 copy-done.4
  19.7 0.0 copy-start.5
  19.7 0.9 copy-done.5
  20.6 0.0 copy-start.6
  20.6 0.9 copy-done.6
  21.5 0.0 copy-start.1
  21.5 0.0 copy-start.3
  21.5 76.0 %shard_map.95.arrived = bf16[4,128,32,128]{3,2,1,0:T(8,128)(2,1)S(1)} custom-call(bf16[2,16,126976]{2,1,0:T(8,128)(2,1)} %volt_far.1, f32[16,4096]{1,0:T(8,128)S(1)} %copy-done, f32[32,8,128]{2,1,0:T(8,128)S(1)} %copy-done.6, f32[32,8,128]{2,1,0:T(8,128)S(1)} %copy-done.5, bf16[256,256]{1,0:T(8,128)(2,1)S(1)} %copy-done.4, bf16[256,256]{1,0:T(8,128)(2,1)S(1)} %copy-done.2), custom_call_target="tpu_custom_call" | custom-call | flops 10000000000 | bytes 16777216 | tf_op jit(solution)/shard_map/pallas_call | solution.py:229
  97.5 0.0 copy-done.1
  97.5 0.0 copy-done.3
  97.6 115.7 %shard_map.96 = (bf16[8,4,2,256,256]{4,3,2,1,0:T(8,128)(2,1)}, bf16[4,2,256,256]{3,2,1,0:T(8,128)(2,1)S(1)}) custom-call(s32[4]{0:T(128)S(1)} %copy-done.1, bf16[4,128,32,128]{3,2,1,0:T(8,128)(2,1)S(1)} %shard_map.95.arrived, s32[256,8]{1,0:T(8,128)S(1)} %bitcast.11, bf16[256,256]{1,0:T(8,128)(2,1)S(1)} %copy-done.3), custom_call_target="tpu_custom_call" | custom-call | flops 10000000000 | bytes 16777216 | tf_op jit(solution)/shard_map/pallas_call | solution.py:337
  213.3 7.8 %copy.20 = bf16[8,1,4,2,256,256]{5,4,3,2,1,0:T(8,128)(2,1)} copy(bf16[8,1,4,2,256,256]{5,4,3,2,1,0:T(8,128)(2,1)} %bitcast.12) | data formatting | bytes 16777216
  221.0 1.0 copy.21
Async XLA Ops:
  16.9 1.0 copy-start
  17.9 0.9 copy-start.2
  18.8 0.9 copy-start.4
  19.7 0.9 copy-start.5
  20.6 0.9 copy-start.6
  21.5 76.0 %copy-start.1 = (s32[4]{0:T(128)S(1)}, s32[4]{0:T(128)}, u32[]{:S(2)}) copy-start(s32[4]{0:T(128)} %lag_table.1) | copy-start | bytes 52
  21.5 76.0 %copy-start.3 = (bf16[256,256]{1,0:T(8,128)(2,1)S(1)}, bf16[256,256]{1,0:T(8,128)(2,1)}, u32[]{:S(2)}) copy-start(bf16[256,256]{1,0:T(8,128)(2,1)} %constant.18.spread) | copy-start | bytes 393220

commit v3 on v2

v3 whole, which is shorter than its diff:
```python
import functools
import math

import jax
import jax.numpy as jnp
import numpy as np
from jax import lax
from jax.experimental import pallas as pl
from jax.experimental.pallas import tpu as pltpu
from jax.sharding import PartitionSpec as P

CH = 4096
TAPS = 16
SPECTRA = 16
COLS = 32
LANES = 128
GROUP = 4
GROUPS = 4


def complex_mul(value, turn):
    real, imag = value
    cos, sin = float(turn.real), float(turn.imag)
    if abs(sin) < 1e-12 and abs(cos - 1) < 1e-12:
        return value
    if abs(cos) < 1e-12 and abs(sin + 1) < 1e-12:
        return (imag, -real)
    if abs(cos + sin) < 1e-12:
        return ((real + imag) * cos, (imag - real) * cos)
    if abs(cos - sin) < 1e-12:
        return ((real - imag) * cos, (real + imag) * cos)
    return (real * cos - imag * sin, real * sin + imag * cos)


def fft_list(values):
    count = len(values)
    if count == 1:
        return values
    if count == 2:
        (ar, ai), (br, bi) = values
        return [(ar + br, ai + bi), (ar - br, ai - bi)]
    if count == 4:
        even = fft_list([values[0], values[2]])
        odd = fft_list([values[1], values[3]])
    else:
        even = fft_list(values[0::2])
        odd = fft_list(values[1::2])
    half = count // 2
    low, high = [], []
    for index in range(half):
        turned = complex_mul(odd[index], np.exp(-2j * np.pi * index / count))
        base = even[index]
        low.append((base[0] + turned[0], base[1] + turned[1]))
        high.append((base[0] - turned[0], base[1] - turned[1]))
    return low + high


def fft_columns(values):
    sections = []
    for low in range(8):
        parts = fft_list([values[8 * high + low] for high in range(4)])
        sections.append([complex_mul(part, np.exp(-2j * np.pi * low * index / 32)) for index, part in enumerate(parts)])
    result = [None] * 32
    for index in range(4):
        parts = fft_list([sections[low][index] for low in range(8)])
        for high in range(8):
            result[index + 4 * high] = parts[high]
    return result


MESH = pl.DeviceIdType.MESH
CONTRACT_LAST = (((1,), (1,)), ((), ()))


def position():
    freq = lax.axis_index("freq")
    blk = lax.axis_index("blk")
    return (lax.rem(blk, 4), lax.rem(freq // 2, 2) * 2 + blk // 4, freq // 4, lax.rem(freq, 2))


def mesh_ids(col, row, layer, core):
    return (layer * 4 + (row // 2) * 2 + core, lax.rem(row, 2) * 4 + col)


def correlator_kernel(
    volt_far, order_row, taps_far, cos_far, sin_far, high_far, low_far, spread_far,
    near, far,
    volt, taps, turn_cos, turn_sin, dft_high, dft_low, spread,
    filt, z_real, z_imag, wide, pieces, arrived, own_order, orders, chosen, natural, rows, tiles, far_tiles,
    load_sem, const_sem, send_sem, recv_sem, own_sem, order_sem, tile_sem,
):
    def load(group):
        first = 0 if isinstance(group, int) else pl.multiple_of((group * GROUP + TAPS - 1) * CH, LANES)
        size = (GROUP + TAPS - 1) * CH if isinstance(group, int) else GROUP * CH
        place = (slice(None), slice(None), pl.ds(first, size))
        return pltpu.make_async_copy(volt_far.at[place], volt.at[place], load_sem.at[group])

    constants = [
        pltpu.make_async_copy(source, place, const_sem.at[index])
        for index, (source, place) in enumerate(
            ((taps_far, taps), (cos_far, turn_cos), (sin_far, turn_sin), (high_far, dft_high), (low_far, dft_low), (spread_far, spread))
        )
    ]
    constants[0].start()
    load(0).start()
    for constant in constants[1:]:
        constant.start()
    for later in range(1, GROUPS):
        load(jnp.int32(later)).start()

    col, row, layer, core = position()
    freq, blk = mesh_ids(col, row, layer, core)
    me = freq * 8 + blk
    side = blk // 4
    parity = lax.rem(blk, 2)

    def target(index):
        step = lax.rem(index * 75, 128)
        return mesh_ids(
            lax.rem(col + lax.rem(step, 4), 4),
            lax.rem(row + lax.rem(step // 4, 4), 4),
            lax.rem(layer + lax.rem(step // 16, 4), 4),
            lax.rem(core + step // 64, 2),
        )

    barrier = pltpu.get_barrier_semaphore()

    def greet(index, carry):
        pl.semaphore_signal(barrier, inc=1, device_id=target(index), device_id_type=MESH)
        return carry

    lax.fori_loop(1, 128, greet, 0)
    own_order[...] = jnp.broadcast_to(order_row[...], (8, 256))
    for constant in constants:
        constant.wait()

    def order_copy(step):
        return pltpu.make_async_remote_copy(
            src_ref=own_order,
            dst_ref=orders.at[blk],
            send_sem=order_sem.at[0],
            recv_sem=order_sem.at[1],
            device_id=(freq, lax.rem(blk + step, 8)),
            device_id_type=MESH,
        )

    def group_step(group, carry):
        @pl.when(group == 0)
        def _():
            load(0).wait()

        @pl.when(group > 0)
        def _():
            load(group).wait()

        def filter_column(index, carry):
            weights = [jnp.broadcast_to(taps[pl.ds(t, 1), pl.ds(pl.multiple_of(index * LANES, LANES), LANES)], (16, LANES)) for t in range(TAPS)]
            for part in range(2):
                frames = []
                for frame in range(GROUP + TAPS - 1):
                    start = pl.multiple_of((group * GROUP + frame) * CH + index * LANES, LANES)
                    frames.append(volt[part, :, pl.ds(start, LANES)].astype(jnp.float32))
                for spec in range(GROUP):
                    total = weights[0] * frames[spec]
                    for tap in range(1, TAPS):
                        total = total + weights[tap] * frames[spec + tap]
                    filt[part, spec, index] = total.astype(jnp.bfloat16)
            return carry

        lax.fori_loop(0, COLS, filter_column, 0)

        for spec in range(GROUP):
            for half in range(2):
                rows_half = slice(half * 8, half * 8 + 8)
                values = []
                for index in range(COLS):
                    values.append(tuple(filt[part, spec, index].astype(jnp.float32)[rows_half] for part in range(2)))
                for index, (real, imag) in enumerate(fft_columns(values)):
                    cos, sin = turn_cos[index], turn_sin[index]
                    place = pl.ds(half * LANES + spec * COLS + index, 8, stride=2 * LANES)
                    z_real[place, :] = real * cos - imag * sin
                    z_imag[place, :] = real * sin + imag * cos

        def last_step(block, carry):
            block_rows = pl.ds(pl.multiple_of(block * 256, 256), 256)
            both = jnp.concatenate([z_real[block_rows, :], z_imag[block_rows, :]], axis=1)
            high = both.astype(jnp.bfloat16)
            low = (both - high.astype(jnp.float32)).astype(jnp.bfloat16)
            total = lax.dot_general(dft_high[...], high, CONTRACT_LAST, preferred_element_type=jnp.float32)
            total = total + lax.dot_general(dft_low[...], high, CONTRACT_LAST, preferred_element_type=jnp.float32)
            total = total + lax.dot_general(dft_high[...], low, CONTRACT_LAST, preferred_element_type=jnp.float32)
            for part in range(2):
                for half in range(2):
                    piece = total[part * 128:part * 128 + 128, half * 128:half * 128 + 128]
                    wide[pl.ds(block * 4 + part * 2 + half, 128, stride=32), :] = piece
            return carry

        lax.fori_loop(0, 8, last_step, 0)

        def narrow(index, carry):
            wide_rows = pl.ds(pl.multiple_of(index * 256, 256), 256)
            pieces[group, pl.ds(index * 8, 8)] = wide[wide_rows, :].astype(jnp.bfloat16).reshape(8, 32, LANES)
            return carry

        lax.fori_loop(0, 16, narrow, 0)

        @pl.when(group == 0)
        def _():
            pl.semaphore_wait(barrier, 127)
            for step in range(1, 8):
                order_copy(step).start()

        def send(index, carry):
            other_freq, other_blk = target(index)
            pltpu.make_async_remote_copy(
                src_ref=pieces.at[group, other_freq * 8 + other_blk],
                dst_ref=arrived.at[group, me],
                send_sem=send_sem.at[group],
                recv_sem=recv_sem.at[group],
                device_id=(other_freq, other_blk),
                device_id_type=MESH,
            ).start()
            return carry

        lax.fori_loop(1, 128, send, 0)
        pltpu.make_async_copy(pieces.at[group, me], arrived.at[group, me], own_sem.at[group]).start()
        return carry

    lax.fori_loop(0, GROUPS, group_step, 0)

    orders[blk] = own_order[...]
    for sem in range(2):
        pltpu.make_async_copy(orders.at[pl.ds(0, 7)], orders.at[pl.ds(0, 7)], order_sem.at[sem]).wait()
    members = lax.broadcasted_iota(jnp.int32, (256, 256), 0)
    for member in range(8):
        flags = (orders[member, 0:1, :] == members).astype(jnp.float32)
        chosen[member] = flags.T.astype(jnp.bfloat16)

    def take_group(group, carry):
        others = pl.ds(0, 127)
        pltpu.make_async_copy(pieces.at[group, me], arrived.at[group, me], own_sem.at[group]).wait()
        pltpu.make_async_copy(pieces.at[group, others], arrived.at[group, others], recv_sem.at[group]).wait()

        def unshuffle(index, carry):
            lanes = jnp.concatenate(
                [arrived[group, pl.ds(pl.multiple_of(index * 16 + step * 8, 8), 8)].reshape(256, LANES) for step in range(2)], axis=1
            )
            sorted_rows = jnp.dot(spread[...], lanes, preferred_element_type=jnp.float32).astype(jnp.bfloat16)
            for member in range(8):
                for part in range(2):
                    start = member * 32 + part * 16
                    for step in range(2):
                        place = pl.ds(pl.multiple_of(index * 32 + step * 16, 16), 16)
                        natural[member, place, part * LANES:part * LANES + LANES] = sorted_rows[start:start + 16, step * LANES:step * LANES + LANES]
            return carry

        lax.fori_loop(0, 8, unshuffle, 0)

        def arrange(member, carry):
            picked = jnp.dot(chosen[member], natural[member], preferred_element_type=jnp.float32).astype(jnp.bfloat16)
            for part in range(2):
                rows[member, part * GROUPS + group] = picked[:, part * LANES:part * LANES + LANES]
            return carry

        lax.fori_loop(0, 8, arrange, 0)
        return carry

    lax.fori_loop(0, GROUPS, take_group, 0)

    def side_of(member, part):
        return jnp.concatenate([rows[member, part * GROUPS + group] for group in range(GROUPS)], axis=1)

    def product(left, right):
        return lax.dot_general(left, right, CONTRACT_LAST, preferred_element_type=jnp.float32)

    def correlate(member, other):
        left_real, left_imag = side_of(member, 0), side_of(member, 1)
        right_real, right_imag = side_of(other, 0), side_of(other, 1)
        real = product(left_real, right_real) + product(left_imag, right_imag)
        imag = product(left_imag, right_real) - product(left_real, right_imag)
        return real * (1.0 / 512), imag * (1.0 / 512)

    def post(is_own, dest, source, place, send, receive, own):
        @pl.when(is_own)
        def _():
            pltpu.make_async_copy(source, place, own).start()

        @pl.when(jnp.logical_not(is_own))
        def _():
            pltpu.make_async_remote_copy(
                src_ref=source, dst_ref=place, send_sem=send, recv_sem=receive, device_id=(freq, dest), device_id_type=MESH
            ).start()

    def turn_target(turn):
        step = lax.rem(turn * 3 + 1, 8)
        return step, lax.rem(side + step // 4, 2) * 4 + lax.rem(col + lax.rem(step, 4), 4)

    def near_step(index, carry):
        lag = index // 8 + 1
        step, dest = turn_target(lax.rem(index, 8))
        values = correlate(dest, lax.rem(dest + lag, 8))
        for part in range(2):
            place = (lag - 1) * 2 + part
            tiles[dest, place] = values[part].astype(jnp.bfloat16)
            post(step == 0, dest, tiles.at[dest, place], near.at[blk, place], tile_sem.at[0], tile_sem.at[1], tile_sem.at[2])
        return carry

    lax.fori_loop(0, 24, near_step, 0)

    def packed_step(index, carry):
        step, dest = turn_target(index)
        real, imag = correlate(dest, dest)
        down = lax.broadcasted_iota(jnp.int32, (256, 256), 0)
        across = lax.broadcasted_iota(jnp.int32, (256, 256), 1)
        tiles[dest, 6] = jnp.where(down >= across, real, imag).astype(jnp.bfloat16)
        post(step == 0, dest, tiles.at[dest, 6], near.at[blk, 6], tile_sem.at[0], tile_sem.at[1], tile_sem.at[2])
        return carry

    lax.fori_loop(0, 8, packed_step, 0)

    def far_step(index, carry):
        dest = parity * 4 + lax.rem(col + index, 4)
        values = correlate(dest, lax.rem(dest + 4, 8))
        for part in range(2):
            far_tiles[index, part] = values[part].astype(jnp.bfloat16)
            post(dest == blk, dest, far_tiles.at[index, part], far.at[blk // 2, part], tile_sem.at[3], tile_sem.at[4], tile_sem.at[5])
        return carry

    lax.fori_loop(0, 4, far_step, 0)

    def finish(group, carry):
        others = pl.ds(0, 127)
        pltpu.make_async_copy(pieces.at[group, others], arrived.at[group, others], send_sem.at[group]).wait()
        return carry

    lax.fori_loop(0, GROUPS, finish, 0)
    pltpu.make_async_copy(tiles.at[0], near.at[0], tile_sem.at[2]).wait()
    for sem in (0, 1):
        pltpu.make_async_copy(tiles.at[pl.ds(0, 7)], near.at[pl.ds(0, 7)], tile_sem.at[sem]).wait()
    has_own = parity == side

    @pl.when(has_own)
    def _():
        pltpu.make_async_copy(far_tiles.at[0], far.at[0], tile_sem.at[5]).wait()
        for sem in (3, 4):
            pltpu.make_async_copy(far_tiles.at[pl.ds(0, 3)], far.at[pl.ds(0, 3)], tile_sem.at[sem]).wait()

    @pl.when(jnp.logical_not(has_own))
    def _():
        for sem in (3, 4):
            pltpu.make_async_copy(far_tiles, far, tile_sem.at[sem]).wait()


def tables():
    rows = np.arange(COLS)[:, None] * np.arange(LANES)[None, :]
    angles = -2.0 * np.pi * rows / CH
    cos = np.repeat(np.cos(angles)[:, None, :], 8, 1) / 64
    sin = np.repeat(np.sin(angles)[:, None, :], 8, 1) / 64
    steps = np.arange(LANES)
    turn = -2.0 * np.pi * (steps[:, None] * steps[None, :] % LANES) / LANES
    dft = np.block([[np.cos(turn), -np.sin(turn)], [np.sin(turn), np.cos(turn)]]).astype(np.float32)
    high = jnp.asarray(dft).astype(jnp.bfloat16)
    low = (jnp.asarray(dft) - high.astype(jnp.float32)).astype(jnp.bfloat16)
    return jnp.asarray(cos, jnp.float32), jnp.asarray(sin, jnp.float32), high, low


def make_tiles(voltages, pfb_taps, order_table):
    cos, sin, high, low = tables()
    constants = [pfb_taps, cos, sin, high, low, spread_table()]
    anywhere = pl.BlockSpec(memory_space=pl.ANY)
    return pl.pallas_call(
        correlator_kernel,
        out_shape=(
            jax.ShapeDtypeStruct((8, 7, 256, 256), jnp.bfloat16),
            jax.ShapeDtypeStruct((4, 2, 256, 256), jnp.bfloat16),
        ),
        in_specs=[anywhere, pl.BlockSpec(memory_space=pltpu.VMEM)] + [pl.BlockSpec(memory_space=pltpu.HBM)] * 6,
        out_specs=(anywhere, anywhere),
        scratch_shapes=[pltpu.VMEM(voltages.shape, jnp.bfloat16)]
        + [pltpu.VMEM(value.shape, value.dtype) for value in constants]
        + [
            pltpu.VMEM((2, GROUP, COLS, 16, LANES), jnp.bfloat16),
            pltpu.VMEM((2048, LANES), jnp.float32),
            pltpu.VMEM((2048, LANES), jnp.float32),
            pltpu.VMEM((4096, LANES), jnp.float32),
            pltpu.VMEM((GROUPS, 128, 32, LANES), jnp.bfloat16),
            pltpu.VMEM((GROUPS, 128, 32, LANES), jnp.bfloat16),
            pltpu.VMEM((8, 256), jnp.int32),
            pltpu.VMEM((8, 8, 256), jnp.int32),
            pltpu.VMEM((8, 256, 256), jnp.bfloat16),
            pltpu.VMEM((8, 256, 256), jnp.bfloat16),
            pltpu.VMEM((8, 8, 256, LANES), jnp.bfloat16),
            pltpu.VMEM((8, 7, 256, 256), jnp.bfloat16),
            pltpu.VMEM((4, 2, 256, 256), jnp.bfloat16),
            pltpu.SemaphoreType.DMA((GROUPS,)),
            pltpu.SemaphoreType.DMA((6,)),
            pltpu.SemaphoreType.DMA((GROUPS,)),
            pltpu.SemaphoreType.DMA((GROUPS,)),
            pltpu.SemaphoreType.DMA((GROUPS,)),
            pltpu.SemaphoreType.DMA((2,)),
            pltpu.SemaphoreType.DMA((6,)),
        ],
        compiler_params=pltpu.CompilerParams(vmem_limit_bytes=42 * 2**20, collective_id=0, has_side_effects=True),
        cost_estimate=pl.CostEstimate(flops=10**10, bytes_accessed=16 * 2**20, transcendentals=0),
    )(voltages, order_table, *constants)


def arrange_kernel(lag_table, near, far, visibility, far_visibility):
    for slot in range(4):
        lag = lag_table[slot]

        @pl.when(lag > 0)
        def _(slot=slot, lag=lag):
            for part in range(2):
                visibility[0, 0, slot, part] = near[0, (lag - 1) * 2 + part]

        @pl.when(lag == 0)
        def _(slot=slot):
            packed = near[0, 6].astype(jnp.float32)
            turned = packed.T
            down = lax.broadcasted_iota(jnp.int32, (256, 256), 0)
            across = lax.broadcasted_iota(jnp.int32, (256, 256), 1)
            visibility[0, 0, slot, 0] = jnp.where(down >= across, packed, turned).astype(jnp.bfloat16)
            mirrored = jnp.where(down > across, -turned, 0.0)
            visibility[0, 0, slot, 1] = jnp.where(down < across, packed, mirrored).astype(jnp.bfloat16)

    far_visibility[0, 0, 0] = far[0, 0]


def arrange(near, far, lag_table):
    return pl.pallas_call(
        arrange_kernel,
        grid=(8,),
        out_shape=(
            jax.ShapeDtypeStruct((8, 1, 4, 2, 256, 256), jnp.bfloat16),
            jax.ShapeDtypeStruct((4, 1, 2, 256, 256), jnp.bfloat16),
        ),
        in_specs=[
            pl.BlockSpec(memory_space=pltpu.SMEM),
            pl.BlockSpec((1, 7, 256, 256), lambda out: (out, 0, 0, 0)),
            pl.BlockSpec((1, 1, 256, 256), lambda out: (out // 2, out % 2, 0, 0)),
        ],
        out_specs=(
            pl.BlockSpec((1, 1, 4, 2, 256, 256), lambda out: (out, 0, 0, 0, 0, 0)),
            pl.BlockSpec((1, 1, 1, 256, 256), lambda out: (out // 2, 0, out % 2, 0, 0)),
        ),
        compiler_params=pltpu.CompilerParams(vmem_limit_bytes=16 * 2**20),
    )(lag_table, near, far)


def per_device(voltages, pfb_taps, order_table, lag_table):
    near, far = make_tiles(voltages, pfb_taps, order_table)
    return arrange(near, far, lag_table)


def spread_table():
    table = np.zeros((256, 256), np.float32)
    for source in range(8):
        for row in range(16):
            for half in range(2):
                table[row * 16 + source * 2 + half, source * 32 + row * 2 + half] = 1
    return jnp.asarray(table).astype(jnp.bfloat16)


def solution(mesh):
    placed = (P(None, ("freq", "blk"), None), P(), P("blk", None), P())
    return jax.shard_map(
        per_device,
        mesh=mesh,
        in_specs=placed,
        out_specs=(P("freq", "blk", None, None, None, None), P("freq", "blk", None, None, None)),
        check_vma=False,
    )
```

time: 224 us -> 194 us (0.87)
  blocking collectives: 16.2 us -> 0 us
  Pallas kernels: 192 us -> 184 us
  local copies, waits for them, and re-layouts: 13.4 us -> 6.15 us
    all_gather x1 -> x0, blocking collectives: 16.2 us -> none  [per_device(): orders = lax.all_gather(order_table, 'blk', axis=0, tiled=True)]
    pallas_call x2, Pallas kernels: 192 us -> 184 us  [the longest x1 178 us: make_tiles(): pl.pallas_call(correlator_kernel, out_shape=(jax.ShapeDtypeStruct((8, 7,...]
    unnamed x16, local copies, waits for them, and re-layouts: 13.3 us -> 6.15 us
where the time goes in v3:
time: 194 us; the launch traced here: 190 us
  Pallas kernels  184 us (95%)
  local copies, waits for them, and re-layouts  6.15 us (3%)
    pallas_call x1, Pallas kernels, make_tiles(): pl.pallas_call(correlator_kernel, out_shape=(jax.ShapeDtypeStruct((8, 7,...  178 us
    unnamed x16, local copies, waits for them, and re-layouts  6.15 us
    pallas_call x1, Pallas kernels, arrange(): pl.pallas_call(arrange_kernel, grid=(8,), out_shape=(jax.ShapeDtypeStruct...  5.94 us

profile of v3, /device:TPU:1, one launch (start us, length us, event | category | flops | bytes accessed | tf_op | source)
XLA Modules:
  0.0 190.5 jit_solution(11112044230531719727)
XLA Ops:
  0.6 0.0 copy-start
  0.6 0.0 copy-start.1
  0.7 0.9 copy-done.1
  1.6 0.0 copy-start.2
  1.6 0.7 copy-done.2
  2.3 0.0 copy-start.3
  2.3 0.9 copy-done.3
  3.2 0.0 copy-start.4
  3.2 0.9 copy-done.4
  4.1 0.0 copy-start.5
  4.1 0.9 copy-done.5
  5.0 0.0 copy-start.6
  5.0 0.9 copy-done.6
  5.9 0.0 copy-start.7
  5.9 0.9 copy-done.7
  6.8 177.7 %shard_map.95 = (bf16[8,7,256,256]{3,2,1,0:T(8,128)(2,1)S(1)}, bf16[4,2,256,256]{3,2,1,0:T(8,128)(2,1)S(1)}) custom-call(bf16[2,16,126976]{2,1,0:T(8,128)(2,1)} %volt_far.1, s32[1,256]{1,0:T(1,128)S(1)} %copy-done.2, f32[16,4096]{1,0:T(8,128)S(1)} %copy-done.1, f32[32,8,128]{2,1,0:T(8,128)S(1)} %copy-done.7, f32[32,8,128]{2,1,0:T(8,128)S(1)} %copy-done.6, ...), custom_call_target="tpu_custom_call" | custom-call | flops 10000000000 | bytes 16777216 | tf_op jit(solution)/shard_map/pallas_call | solution.py:371
  184.5 0.0 copy-done
  184.5 5.9 %shard_map.96 = (bf16[8,1,4,2,256,256]{5,4,3,2,1,0:T(8,128)(2,1)}, bf16[4,1,2,256,256]{4,3,2,1,0:T(8,128)(2,1)}) custom-call(s32[4]{0:T(128)S(1)} %copy-done, bf16[8,7,256,256]{3,2,1,0:T(8,128)(2,1)S(1)} %get-tuple-element.4.near, bf16[4,2,256,256]{3,2,1,0:T(8,128)(2,1)S(1)} %get-tuple-element.5.far), custom_call_target="tpu_custom_call" | custom-call | tf_op jit(solution)/shard_map/pallas_call | solution.py:431
Async XLA Ops:
  0.6 183.9 %copy-start = (s32[4]{0:T(128)S(1)}, s32[4]{0:T(128)}, u32[]{:S(2)}) copy-start(s32[4]{0:T(128)} %lag_table.1) | copy-start | bytes 52
  0.6 1.0 copy-start.1
  1.6 0.7 copy-start.2
  2.3 0.9 copy-start.3
  3.2 0.9 copy-start.4
  4.1 0.9 copy-start.5
  5.0 0.9 copy-start.6
  5.9 0.9 copy-start.7

commit v4 on v3

--- a/solution.py
+++ b/solution.py
@@ -16,6 +16,8 @@
 LANES = 128
 GROUP = 4
 GROUPS = 4
+Z_STRIDE = 264
+WIDE_STRIDE = 40
 
 
 def complex_mul(value, turn):
@@ -83,11 +85,11 @@
 
 
 def correlator_kernel(
-    volt_far, order_row, taps_far, cos_far, sin_far, high_far, low_far, spread_far,
+    volt_far, order_row, taps, numbers,
     near, far,
-    volt, taps, turn_cos, turn_sin, dft_high, dft_low, spread,
+    volt, turn_cos, turn_sin, dft_high, dft_low, spread,
     filt, z_real, z_imag, wide, pieces, arrived, own_order, orders, chosen, natural, rows, tiles, far_tiles,
-    load_sem, const_sem, send_sem, recv_sem, own_sem, order_sem, tile_sem,
+    load_sem, send_sem, recv_sem, own_sem, order_sem, tile_sem,
 ):
     def load(group):
         first = 0 if isinstance(group, int) else pl.multiple_of((group * GROUP + TAPS - 1) * CH, LANES)
@@ -95,16 +97,7 @@
         place = (slice(None), slice(None), pl.ds(first, size))
         return pltpu.make_async_copy(volt_far.at[place], volt.at[place], load_sem.at[group])
 
-    constants = [
-        pltpu.make_async_copy(source, place, const_sem.at[index])
-        for index, (source, place) in enumerate(
-            ((taps_far, taps), (cos_far, turn_cos), (sin_far, turn_sin), (high_far, dft_high), (low_far, dft_low), (spread_far, spread))
-        )
-    ]
-    constants[0].start()
     load(0).start()
-    for constant in constants[1:]:
-        constant.start()
     for later in range(1, GROUPS):
         load(jnp.int32(later)).start()
 
@@ -112,27 +105,45 @@
     freq, blk = mesh_ids(col, row, layer, core)
     me = freq * 8 + blk
     side = blk // 4
-    parity = lax.rem(blk, 2)
-
-    def target(index):
-        step = lax.rem(index * 75, 128)
-        return mesh_ids(
-            lax.rem(col + lax.rem(step, 4), 4),
-            lax.rem(row + lax.rem(step // 4, 4), 4),
-            lax.rem(layer + lax.rem(step // 16, 4), 4),
-            lax.rem(core + step // 64, 2),
-        )
+    channel = col * 2 + side
+
+    def visit_others(visit):
+        cols = [lax.rem(col + step, 4) for step in range(4)]
+
+        def visit_plane(index, carry):
+            new_row = lax.rem(row + lax.rem(index, 4), 4)
+            new_layer = lax.rem(layer + lax.rem(lax.div(index, 4), 4), 4)
+            new_core = lax.rem(core + lax.div(index, 16), 2)
+            other_freq = new_layer * 4 + lax.div(new_row, 2) * 2 + new_core
+            other_side = lax.rem(new_row, 2)
+
+            @pl.when(index > 0)
+            def _():
+                visit(other_freq, other_side, cols[0])
+
+            for step in range(1, 4):
+                visit(other_freq, other_side, cols[step])
+            return carry
+
+        lax.fori_loop(0, 32, visit_plane, 0)
 
     barrier = pltpu.get_barrier_semaphore()
 
-    def greet(index, carry):
-        pl.semaphore_signal(barrier, inc=1, device_id=target(index), device_id_type=MESH)
-        return carry
-
-    lax.fori_loop(1, 128, greet, 0)
+    def greet(other_freq, other_side, other_col):
+        pl.semaphore_signal(barrier, inc=1, device_id=(other_freq, other_side * 4 + other_col), device_id_type=MESH)
+
+    visit_others(greet)
     own_order[...] = jnp.broadcast_to(order_row[...], (8, 256))
-    for constant in constants:
-        constant.wait()
+    for index in range(COLS):
+        turn_cos[index] = jnp.broadcast_to(numbers[index:index + 1, :], (8, LANES))
+        turn_sin[index] = jnp.broadcast_to(numbers[COLS + index:COLS + index + 1, :], (8, LANES))
+    dft = jnp.concatenate([numbers[2 * COLS:2 * COLS + 256, :], numbers[2 * COLS + 256:2 * COLS + 512, :]], axis=1)
+    dft_high[...] = dft.astype(jnp.bfloat16)
+    dft_low[...] = (dft - dft.astype(jnp.bfloat16).astype(jnp.float32)).astype(jnp.bfloat16)
+    sorted_row = lax.broadcasted_iota(jnp.int32, (256, 256), 0)
+    came_row = lax.broadcasted_iota(jnp.int32, (256, 256), 1)
+    wanted = jnp.bitwise_and(sorted_row, 14) * 16 + lax.shift_right_logical(sorted_row, 4) * 2 + jnp.bitwise_and(sorted_row, 1)
+    spread[...] = (wanted == came_row).astype(jnp.float32).astype(jnp.bfloat16)
 
     def order_copy(step):
         return pltpu.make_async_remote_copy(
@@ -164,7 +175,7 @@
                     total = weights[0] * frames[spec]
                     for tap in range(1, TAPS):
                         total = total + weights[tap] * frames[spec + tap]
-                    filt[part, spec, index] = total.astype(jnp.bfloat16)
+                    filt[part, spec, index] = total.astype(jnp.bfloat16).astype(jnp.float32)
             return carry
 
         lax.fori_loop(0, COLS, filter_column, 0)
@@ -174,15 +185,15 @@
                 rows_half = slice(half * 8, half * 8 + 8)
                 values = []
                 for index in range(COLS):
-                    values.append(tuple(filt[part, spec, index].astype(jnp.float32)[rows_half] for part in range(2)))
+                    values.append(tuple(filt[part, spec, index, rows_half] for part in range(2)))
                 for index, (real, imag) in enumerate(fft_columns(values)):
                     cos, sin = turn_cos[index], turn_sin[index]
-                    place = pl.ds(half * LANES + spec * COLS + index, 8, stride=2 * LANES)
+                    place = pl.ds(half * LANES + spec * COLS + index, 8, stride=Z_STRIDE)
                     z_real[place, :] = real * cos - imag * sin
                     z_imag[place, :] = real * sin + imag * cos
 
         def last_step(block, carry):
-            block_rows = pl.ds(pl.multiple_of(block * 256, 256), 256)
+            block_rows = pl.ds(pl.multiple_of(block * Z_STRIDE, 8), 256)
             both = jnp.concatenate([z_real[block_rows, :], z_imag[block_rows, :]], axis=1)
             high = both.astype(jnp.bfloat16)
             low = (both - high.astype(jnp.float32)).astype(jnp.bfloat16)
@@ -192,14 +203,15 @@
             for part in range(2):
                 for half in range(2):
                     piece = total[part * 128:part * 128 + 128, half * 128:half * 128 + 128]
-                    wide[pl.ds(block * 4 + part * 2 + half, 128, stride=32), :] = piece
-            return carry
-
-        lax.fori_loop(0, 8, last_step, 0)
+                    wide[pl.ds(block * 4 + part * 2 + half, 128, stride=WIDE_STRIDE), :] = piece
+            return carry
+
+        lax.fori_loop(0, 8, last_step, 0, unroll=2)
 
         def narrow(index, carry):
-            wide_rows = pl.ds(pl.multiple_of(index * 256, 256), 256)
-            pieces[group, pl.ds(index * 8, 8)] = wide[wide_rows, :].astype(jnp.bfloat16).reshape(8, 32, LANES)
+            for sub in range(8):
+                wide_rows = pl.ds(pl.multiple_of((index * 8 + sub) * WIDE_STRIDE, 8), 32)
+                pieces[group, index * 8 + sub] = wide[wide_rows, :].astype(jnp.bfloat16)
             return carry
 
         lax.fori_loop(0, 16, narrow, 0)
@@ -210,20 +222,18 @@
             for step in range(1, 8):
                 order_copy(step).start()
 
-        def send(index, carry):
-            other_freq, other_blk = target(index)
+        def send(other_freq, other_side, other_col):
             pltpu.make_async_remote_copy(
-                src_ref=pieces.at[group, other_freq * 8 + other_blk],
+                src_ref=pieces.at[group, other_freq * 8 + other_col * 2 + other_side],
                 dst_ref=arrived.at[group, me],
                 send_sem=send_sem.at[group],
                 recv_sem=recv_sem.at[group],
-                device_id=(other_freq, other_blk),
+                device_id=(other_freq, other_side * 4 + other_col),
                 device_id_type=MESH,
             ).start()
-            return carry
-
-        lax.fori_loop(1, 128, send, 0)
-        pltpu.make_async_copy(pieces.at[group, me], arrived.at[group, me], own_sem.at[group]).start()
+
+        visit_others(send)
+        pltpu.make_async_copy(pieces.at[group, freq * 8 + channel], arrived.at[group, me], own_sem.at[group]).start()
         return carry
 
     lax.fori_loop(0, GROUPS, group_step, 0)
@@ -238,7 +248,7 @@
 
     def take_group(group, carry):
         others = pl.ds(0, 127)
-        pltpu.make_async_copy(pieces.at[group, me], arrived.at[group, me], own_sem.at[group]).wait()
+        pltpu.make_async_copy(pieces.at[group, freq * 8 + channel], arrived.at[group, me], own_sem.at[group]).wait()
         pltpu.make_async_copy(pieces.at[group, others], arrived.at[group, others], recv_sem.at[group]).wait()
 
         def unshuffle(index, carry):
@@ -254,7 +264,7 @@
                         natural[member, place, part * LANES:part * LANES + LANES] = sorted_rows[start:start + 16, step * LANES:step * LANES + LANES]
             return carry
 
-        lax.fori_loop(0, 8, unshuffle, 0)
+        lax.fori_loop(0, 8, unshuffle, 0, unroll=4)
 
         def arrange(member, carry):
             picked = jnp.dot(chosen[member], natural[member], preferred_element_type=jnp.float32).astype(jnp.bfloat16)
@@ -262,7 +272,7 @@
                 rows[member, part * GROUPS + group] = picked[:, part * LANES:part * LANES + LANES]
             return carry
 
-        lax.fori_loop(0, 8, arrange, 0)
+        lax.fori_loop(0, 8, arrange, 0, unroll=4)
         return carry
 
     lax.fori_loop(0, GROUPS, take_group, 0)
@@ -302,7 +312,7 @@
         for part in range(2):
             place = (lag - 1) * 2 + part
             tiles[dest, place] = values[part].astype(jnp.bfloat16)
-            post(step == 0, dest, tiles.at[dest, place], near.at[blk, place], tile_sem.at[0], tile_sem.at[1], tile_sem.at[2])
+            post(step == 0, dest, tiles.at[dest, place], near.at[channel, place], tile_sem.at[0], tile_sem.at[1], tile_sem.at[2])
         return carry
 
     lax.fori_loop(0, 24, near_step, 0)
@@ -313,17 +323,18 @@
         down = lax.broadcasted_iota(jnp.int32, (256, 256), 0)
         across = lax.broadcasted_iota(jnp.int32, (256, 256), 1)
         tiles[dest, 6] = jnp.where(down >= across, real, imag).astype(jnp.bfloat16)
-        post(step == 0, dest, tiles.at[dest, 6], near.at[blk, 6], tile_sem.at[0], tile_sem.at[1], tile_sem.at[2])
+        post(step == 0, dest, tiles.at[dest, 6], near.at[channel, 6], tile_sem.at[0], tile_sem.at[1], tile_sem.at[2])
         return carry
 
     lax.fori_loop(0, 8, packed_step, 0)
 
     def far_step(index, carry):
-        dest = parity * 4 + lax.rem(col + index, 4)
+        step = lax.rem(index + 1, 4)
+        dest = side * 4 + lax.rem(col + step, 4)
         values = correlate(dest, lax.rem(dest + 4, 8))
         for part in range(2):
             far_tiles[index, part] = values[part].astype(jnp.bfloat16)
-            post(dest == blk, dest, far_tiles.at[index, part], far.at[blk // 2, part], tile_sem.at[3], tile_sem.at[4], tile_sem.at[5])
+            post(step == 0, dest, far_tiles.at[index, part], far.at[col, part], tile_sem.at[3], tile_sem.at[4], tile_sem.at[5])
         return carry
 
     lax.fori_loop(0, 4, far_step, 0)
@@ -337,36 +348,22 @@
     pltpu.make_async_copy(tiles.at[0], near.at[0], tile_sem.at[2]).wait()
     for sem in (0, 1):
         pltpu.make_async_copy(tiles.at[pl.ds(0, 7)], near.at[pl.ds(0, 7)], tile_sem.at[sem]).wait()
-    has_own = parity == side
-
-    @pl.when(has_own)
-    def _():
-        pltpu.make_async_copy(far_tiles.at[0], far.at[0], tile_sem.at[5]).wait()
-        for sem in (3, 4):
-            pltpu.make_async_copy(far_tiles.at[pl.ds(0, 3)], far.at[pl.ds(0, 3)], tile_sem.at[sem]).wait()
-
-    @pl.when(jnp.logical_not(has_own))
-    def _():
-        for sem in (3, 4):
-            pltpu.make_async_copy(far_tiles, far, tile_sem.at[sem]).wait()
+    pltpu.make_async_copy(far_tiles.at[0], far.at[0], tile_sem.at[5]).wait()
+    for sem in (3, 4):
+        pltpu.make_async_copy(far_tiles.at[pl.ds(0, 3)], far.at[pl.ds(0, 3)], tile_sem.at[sem]).wait()
 
 
 def tables():
     rows = np.arange(COLS)[:, None] * np.arange(LANES)[None, :]
     angles = -2.0 * np.pi * rows / CH
-    cos = np.repeat(np.cos(angles)[:, None, :], 8, 1) / 64
-    sin = np.repeat(np.sin(angles)[:, None, :], 8, 1) / 64
     steps = np.arange(LANES)
     turn = -2.0 * np.pi * (steps[:, None] * steps[None, :] % LANES) / LANES
-    dft = np.block([[np.cos(turn), -np.sin(turn)], [np.sin(turn), np.cos(turn)]]).astype(np.float32)
-    high = jnp.asarray(dft).astype(jnp.bfloat16)
-    low = (jnp.asarray(dft) - high.astype(jnp.float32)).astype(jnp.bfloat16)
-    return jnp.asarray(cos, jnp.float32), jnp.asarray(sin, jnp.float32), high, low
+    dft = np.block([[np.cos(turn), -np.sin(turn)], [np.sin(turn), np.cos(turn)]])
+    parts = [np.cos(angles) / 64, np.sin(angles) / 64, dft[:, :LANES], dft[:, LANES:]]
+    return jnp.asarray(np.concatenate(parts, axis=0), jnp.float32)
 
 
 def make_tiles(voltages, pfb_taps, order_table):
-    cos, sin, high, low = tables()
-    constants = [pfb_taps, cos, sin, high, low, spread_table()]
     anywhere = pl.BlockSpec(memory_space=pl.ANY)
     return pl.pallas_call(
         correlator_kernel,
@@ -374,15 +371,19 @@
             jax.ShapeDtypeStruct((8, 7, 256, 256), jnp.bfloat16),
             jax.ShapeDtypeStruct((4, 2, 256, 256), jnp.bfloat16),
         ),
-        in_specs=[anywhere, pl.BlockSpec(memory_space=pltpu.VMEM)] + [pl.BlockSpec(memory_space=pltpu.HBM)] * 6,
+        in_specs=[anywhere] + [pl.BlockSpec(memory_space=pltpu.VMEM)] * 3,
         out_specs=(anywhere, anywhere),
         scratch_shapes=[pltpu.VMEM(voltages.shape, jnp.bfloat16)]
-        + [pltpu.VMEM(value.shape, value.dtype) for value in constants]
         + [
-            pltpu.VMEM((2, GROUP, COLS, 16, LANES), jnp.bfloat16),
-            pltpu.VMEM((2048, LANES), jnp.float32),
-            pltpu.VMEM((2048, LANES), jnp.float32),
-            pltpu.VMEM((4096, LANES), jnp.float32),
+            pltpu.VMEM((COLS, 8, LANES), jnp.float32),
+            pltpu.VMEM((COLS, 8, LANES), jnp.float32),
+            pltpu.VMEM((256, 256), jnp.bfloat16),
+            pltpu.VMEM((256, 256), jnp.bfloat16),
+            pltpu.VMEM((256, 256), jnp.bfloat16),
+            pltpu.VMEM((2, GROUP, COLS, 16, LANES), jnp.float32),
+            pltpu.VMEM((8 * Z_STRIDE, LANES), jnp.float32),
+            pltpu.VMEM((8 * Z_STRIDE, LANES), jnp.float32),
+            pltpu.VMEM((128 * WIDE_STRIDE, LANES), jnp.float32),
             pltpu.VMEM((GROUPS, 128, 32, LANES), jnp.bfloat16),
             pltpu.VMEM((GROUPS, 128, 32, LANES), jnp.bfloat16),
             pltpu.VMEM((8, 256), jnp.int32),
@@ -393,7 +394,6 @@
             pltpu.VMEM((8, 7, 256, 256), jnp.bfloat16),
             pltpu.VMEM((4, 2, 256, 256), jnp.bfloat16),
             pltpu.SemaphoreType.DMA((GROUPS,)),
-            pltpu.SemaphoreType.DMA((6,)),
             pltpu.SemaphoreType.DMA((GROUPS,)),
             pltpu.SemaphoreType.DMA((GROUPS,)),
             pltpu.SemaphoreType.DMA((GROUPS,)),
@@ -402,48 +402,54 @@
         ],
         compiler_params=pltpu.CompilerParams(vmem_limit_bytes=42 * 2**20, collective_id=0, has_side_effects=True),
         cost_estimate=pl.CostEstimate(flops=10**10, bytes_accessed=16 * 2**20, transcendentals=0),
-    )(voltages, order_table, *constants)
-
-
-def arrange_kernel(lag_table, near, far, visibility, far_visibility):
+    )(voltages, order_table, pfb_taps, tables())
+
+
+def arrange_kernel(lag_table, near, far, visibility, far_visibility, unpacked, sems):
+    far_copy = pltpu.make_async_copy(far, far_visibility.at[:, 0], sems.at[0])
+    far_copy.start()
     for slot in range(4):
         lag = lag_table[slot]
 
         @pl.when(lag > 0)
         def _(slot=slot, lag=lag):
-            for part in range(2):
-                visibility[0, 0, slot, part] = near[0, (lag - 1) * 2 + part]
-
-        @pl.when(lag == 0)
+            pltpu.make_async_copy(near.at[:, pl.ds((lag - 1) * 2, 2)], visibility.at[:, 0, slot], sems.at[1]).start()
+
+    own_slot = 0
+    for slot in range(4):
+        own_slot = jnp.where(lag_table[slot] == 0, slot, own_slot)
+    down = lax.broadcasted_iota(jnp.int32, (256, 256), 0)
+    across = lax.broadcasted_iota(jnp.int32, (256, 256), 1)
+
+    def unpack(out, carry):
+        packed = near[out, 6].astype(jnp.float32)
+        turned = packed.T
+        unpacked[out, 0] = jnp.where(down >= across, packed, turned).astype(jnp.bfloat16)
+        mirrored = jnp.where(down > across, -turned, 0.0)
+        unpacked[out, 1] = jnp.where(down < across, packed, mirrored).astype(jnp.bfloat16)
+        pltpu.make_async_copy(unpacked.at[out], visibility.at[out, 0, own_slot], sems.at[2]).start()
+        return carry
+
+    lax.fori_loop(0, 8, unpack, 0)
+    far_copy.wait()
+    for slot in range(4):
+        @pl.when(lag_table[slot] > 0)
         def _(slot=slot):
-            packed = near[0, 6].astype(jnp.float32)
-            turned = packed.T
-            down = lax.broadcasted_iota(jnp.int32, (256, 256), 0)
-            across = lax.broadcasted_iota(jnp.int32, (256, 256), 1)
-            visibility[0, 0, slot, 0] = jnp.where(down >= across, packed, turned).astype(jnp.bfloat16)
-            mirrored = jnp.where(down > across, -turned, 0.0)
-            visibility[0, 0, slot, 1] = jnp.where(down < across, packed, mirrored).astype(jnp.bfloat16)
-
-    far_visibility[0, 0, 0] = far[0, 0]
+            pltpu.make_async_copy(near.at[:, pl.ds(0, 2)], visibility.at[:, 0, slot], sems.at[1]).wait()
+
+    pltpu.make_async_copy(unpacked, visibility.at[:, 0, 0], sems.at[2]).wait()
 
 
 def arrange(near, far, lag_table):
     return pl.pallas_call(
         arrange_kernel,
-        grid=(8,),
         out_shape=(
             jax.ShapeDtypeStruct((8, 1, 4, 2, 256, 256), jnp.bfloat16),
             jax.ShapeDtypeStruct((4, 1, 2, 256, 256), jnp.bfloat16),
         ),
-        in_specs=[
-            pl.BlockSpec(memory_space=pltpu.SMEM),
-            pl.BlockSpec((1, 7, 256, 256), lambda out: (out, 0, 0, 0)),
-            pl.BlockSpec((1, 1, 256, 256), lambda out: (out // 2, out % 2, 0, 0)),
-        ],
-        out_specs=(
-            pl.BlockSpec((1, 1, 4, 2, 256, 256), lambda out: (out, 0, 0, 0, 0, 0)),
-            pl.BlockSpec((1, 1, 1, 256, 256), lambda out: (out // 2, 0, out % 2, 0, 0)),
-        ),
+        in_specs=[pl.BlockSpec(memory_space=pltpu.SMEM), pl.BlockSpec(memory_space=pltpu.VMEM), pl.BlockSpec(memory_space=pltpu.VMEM)],
+        out_specs=(pl.BlockSpec(memory_space=pl.ANY), pl.BlockSpec(memory_space=pl.ANY)),
+        scratch_shapes=[pltpu.VMEM((8, 2, 256, 256), jnp.bfloat16), pltpu.SemaphoreType.DMA((3,))],
         compiler_params=pltpu.CompilerParams(vmem_limit_bytes=16 * 2**20),
     )(lag_table, near, far)
 
@@ -451,15 +457,6 @@
 def per_device(voltages, pfb_taps, order_table, lag_table):
     near, far = make_tiles(voltages, pfb_taps, order_table)
     return arrange(near, far, lag_table)
-
-
-def spread_table():
-    table = np.zeros((256, 256), np.float32)
-    for source in range(8):
-        for row in range(16):
-            for half in range(2):
-                table[row * 16 + source * 2 + half, source * 32 + row * 2 + half] = 1
-    return jnp.asarray(table).astype(jnp.bfloat16)
 
 
 def solution(mesh):

time: 194 us -> 165 us (0.85); the launches traced: 190 us -> 165 us
  Pallas kernels: 184 us -> 162 us
  local copies, waits for them, and re-layouts: 6.15 us -> 2.59 us
    pallas_call x1, Pallas kernels: 178 us -> 158 us  [make_tiles(): pl.pallas_call(correlator_kernel, out_shape=(jax.ShapeDtypeStruct((8, 7,...]
    unnamed x16 -> x8, local copies, waits for them, and re-layouts: 6.15 us -> 2.59 us
where the time goes in v4:
time: 165 us
  Pallas kernels  162 us (98%)
  local copies, waits for them, and re-layouts  2.59 us (2%)
    pallas_call x1, Pallas kernels, make_tiles(): pl.pallas_call(correlator_kernel, out_shape=(jax.ShapeDtypeStruct((8, 7,...  158 us
    pallas_call x1, Pallas kernels, arrange(): pl.pallas_call(arrange_kernel, out_shape=(jax.ShapeDtypeStruct((8, 1, 4,...  4.17 us

profile of v4, /device:TPU:1, one launch (start us, length us, event | category | flops | bytes accessed | tf_op | source)
XLA Modules:
  0.0 165.1 jit_solution(316143105148890115)
XLA Ops:
  0.6 0.0 copy-start
  0.6 0.0 copy-start.1
  0.7 0.9 copy-done.1
  1.6 0.0 copy-start.2
  1.6 0.7 copy-done.2
  2.3 0.0 copy-start.3
  2.3 1.0 copy-done.3
  3.2 157.7 %shard_map.68 = (bf16[8,7,256,256]{3,2,1,0:T(8,128)(2,1)S(1)}, bf16[4,2,256,256]{3,2,1,0:T(8,128)(2,1)S(1)}) custom-call(bf16[2,16,126976]{2,1,0:T(8,128)(2,1)} %volt_far.1, s32[1,256]{1,0:T(1,128)S(1)} %copy-done.2, f32[16,4096]{1,0:T(8,128)S(1)} %copy-done.1, f32[576,128]{1,0:T(8,128)S(1)} %copy-done.3), custom_call_target="tpu_custom_call" | custom-call | flops 10000000000 | bytes 16777216 | tf_op jit(solution)/shard_map/pallas_call | solution.py:368
  160.9 0.0 copy-done
  160.9 4.2 %shard_map.69 = (bf16[8,1,4,2,256,256]{5,4,3,2,1,0:T(8,128)(2,1)}, bf16[4,1,2,256,256]{4,3,2,1,0:T(8,128)(2,1)}) custom-call(s32[4]{0:T(128)S(1)} %copy-done, bf16[8,7,256,256]{3,2,1,0:T(8,128)(2,1)S(1)} %get-tuple-element.4.near, bf16[4,2,256,256]{3,2,1,0:T(8,128)(2,1)S(1)} %get-tuple-element.5.far), custom_call_target="tpu_custom_call" | custom-call | tf_op jit(solution)/shard_map/pallas_call | solution.py:444
Async XLA Ops:
  0.6 160.3 %copy-start = (s32[4]{0:T(128)S(1)}, s32[4]{0:T(128)}, u32[]{:S(2)}) copy-start(s32[4]{0:T(128)} %lag_table.1) | copy-start | bytes 52
  0.6 1.0 copy-start.1
  1.6 0.7 copy-start.2
  2.3 1.0 copy-start.3

commit v5 on v4

--- a/solution.py
+++ b/solution.py
@@ -16,6 +16,7 @@
 LANES = 128
 GROUP = 4
 GROUPS = 4
+WHOLE_GROUPS = 1
 Z_STRIDE = 264
 WIDE_STRIDE = 40
 
@@ -86,9 +87,9 @@
 
 def correlator_kernel(
     volt_far, order_row, taps, numbers,
-    near, far,
+    near, mirror, far,
     volt, turn_cos, turn_sin, dft_high, dft_low, spread,
-    filt, z_real, z_imag, wide, pieces, arrived, own_order, orders, chosen, natural, rows, tiles, far_tiles,
+    filt, z_real, z_imag, wide, pieces, arrived, own_order, orders, chosen, natural, rows, tiles, far_tiles, packed, unpacked,
     load_sem, send_sem, recv_sem, own_sem, order_sem, tile_sem,
 ):
     def load(group):
@@ -142,7 +143,7 @@
     dft_low[...] = (dft - dft.astype(jnp.bfloat16).astype(jnp.float32)).astype(jnp.bfloat16)
     sorted_row = lax.broadcasted_iota(jnp.int32, (256, 256), 0)
     came_row = lax.broadcasted_iota(jnp.int32, (256, 256), 1)
-    wanted = jnp.bitwise_and(sorted_row, 14) * 16 + lax.shift_right_logical(sorted_row, 4) * 2 + jnp.bitwise_and(sorted_row, 1)
+    wanted = jnp.bitwise_and(sorted_row, 30) * 8 + lax.shift_right_logical(sorted_row, 5) * 2 + jnp.bitwise_and(sorted_row, 1)
     spread[...] = (wanted == came_row).astype(jnp.float32).astype(jnp.bfloat16)
 
     def order_copy(step):
@@ -154,6 +155,29 @@
             device_id=(freq, lax.rem(blk + step, 8)),
             device_id_type=MESH,
         )
+
+    def half_rows(half):
+        return pl.ds(pl.multiple_of(half * 16, 16), 16)
+
+    first = lax.rem(side + core, 2)
+    second = 1 - first
+
+    def send_piece(group, part, half, other_freq, other_side, other_col):
+        pltpu.make_async_remote_copy(
+            src_ref=pieces.at[group, other_freq * 8 + other_col * 2 + other_side, part],
+            dst_ref=arrived.at[group, me, part],
+            send_sem=send_sem.at[half, group],
+            recv_sem=recv_sem.at[half, group],
+            device_id=(other_freq, other_side * 4 + other_col),
+            device_id_type=MESH,
+        ).start()
+
+    def own_piece(group):
+        return pltpu.make_async_copy(pieces.at[group, freq * 8 + channel], arrived.at[group, me], own_sem.at[group])
+
+    def wait_pieces(group, part, half, sems):
+        place = (group, pl.ds(0, 127), part)
+        pltpu.make_async_copy(pieces.at[place], arrived.at[place], sems.at[half, group]).wait()
 
     def group_step(group, carry):
         @pl.when(group == 0)
@@ -222,21 +246,33 @@
             for step in range(1, 8):
                 order_copy(step).start()
 
+        @pl.when(group < WHOLE_GROUPS)
+        def _():
+            def send(other_freq, other_side, other_col):
+                send_piece(group, slice(None), 0, other_freq, other_side, other_col)
+
+            visit_others(send)
+
+        @pl.when(group >= WHOLE_GROUPS)
+        def _():
+            def send(other_freq, other_side, other_col):
+                send_piece(group, half_rows(lax.rem(other_side + lax.rem(other_freq, 2), 2)), 0, other_freq, other_side, other_col)
+
+            visit_others(send)
+
+        own_piece(group).start()
+        return carry
+
+    lax.fori_loop(0, GROUPS, group_step, 0)
+
+    def send_rest(group, carry):
         def send(other_freq, other_side, other_col):
-            pltpu.make_async_remote_copy(
-                src_ref=pieces.at[group, other_freq * 8 + other_col * 2 + other_side],
-                dst_ref=arrived.at[group, me],
-                send_sem=send_sem.at[group],
-                recv_sem=recv_sem.at[group],
-                device_id=(other_freq, other_side * 4 + other_col),
-                device_id_type=MESH,
-            ).start()
+            send_piece(group, half_rows(lax.rem(1 + other_side + lax.rem(other_freq, 2), 2)), 1, other_freq, other_side, other_col)
 
         visit_others(send)
-        pltpu.make_async_copy(pieces.at[group, freq * 8 + channel], arrived.at[group, me], own_sem.at[group]).start()
-        return carry
-
-    lax.fori_loop(0, GROUPS, group_step, 0)
+        return carry
+
+    lax.fori_loop(WHOLE_GROUPS, GROUPS, send_rest, 0)
 
     orders[blk] = own_order[...]
     for sem in range(2):
@@ -246,36 +282,51 @@
         flags = (orders[member, 0:1, :] == members).astype(jnp.float32)
         chosen[member] = flags.T.astype(jnp.bfloat16)
 
-    def take_group(group, carry):
-        others = pl.ds(0, 127)
-        pltpu.make_async_copy(pieces.at[group, freq * 8 + channel], arrived.at[group, me], own_sem.at[group]).wait()
-        pltpu.make_async_copy(pieces.at[group, others], arrived.at[group, others], recv_sem.at[group]).wait()
-
+    def take_half(group, half):
         def unshuffle(index, carry):
             lanes = jnp.concatenate(
-                [arrived[group, pl.ds(pl.multiple_of(index * 16 + step * 8, 8), 8)].reshape(256, LANES) for step in range(2)], axis=1
+                [
+                    arrived[group, pl.ds(pl.multiple_of(index * 32 + step * 16, 16), 16), half_rows(half)].reshape(256, LANES)
+                    for step in range(2)
+                ],
+                axis=1,
             )
             sorted_rows = jnp.dot(spread[...], lanes, preferred_element_type=jnp.float32).astype(jnp.bfloat16)
-            for member in range(8):
+            for member in range(4):
                 for part in range(2):
-                    start = member * 32 + part * 16
+                    start = member * 64 + part * 32
                     for step in range(2):
-                        place = pl.ds(pl.multiple_of(index * 32 + step * 16, 16), 16)
-                        natural[member, place, part * LANES:part * LANES + LANES] = sorted_rows[start:start + 16, step * LANES:step * LANES + LANES]
+                        place = pl.ds(pl.multiple_of(index * 64 + step * 32, 32), 32)
+                        natural[half * 4 + member, place, part * LANES:part * LANES + LANES] = sorted_rows[start:start + 32, step * LANES:step * LANES + LANES]
             return carry
 
-        lax.fori_loop(0, 8, unshuffle, 0, unroll=4)
-
-        def arrange(member, carry):
+        lax.fori_loop(0, 4, unshuffle, 0, unroll=4)
+
+        def arrange(index, carry):
+            member = half * 4 + index
             picked = jnp.dot(chosen[member], natural[member], preferred_element_type=jnp.float32).astype(jnp.bfloat16)
             for part in range(2):
                 rows[member, part * GROUPS + group] = picked[:, part * LANES:part * LANES + LANES]
             return carry
 
-        lax.fori_loop(0, 8, arrange, 0, unroll=4)
-        return carry
-
-    lax.fori_loop(0, GROUPS, take_group, 0)
+        lax.fori_loop(0, 4, arrange, 0, unroll=4)
+
+    def take_whole(group, carry):
+        own_piece(group).wait()
+        wait_pieces(group, slice(None), 0, recv_sem)
+        for half in range(2):
+            take_half(group, half)
+        return carry
+
+    lax.fori_loop(0, WHOLE_GROUPS, take_whole, 0)
+
+    def take_first(group, carry):
+        own_piece(group).wait()
+        wait_pieces(group, pl.ds(0, 16), 0, recv_sem)
+        take_half(group, first)
+        return carry
+
+    lax.fori_loop(WHOLE_GROUPS, GROUPS, take_first, 0)
 
     def side_of(member, part):
         return jnp.concatenate([rows[member, part * GROUPS + group] for group in range(GROUPS)], axis=1)
@@ -305,28 +356,64 @@
         step = lax.rem(turn * 3 + 1, 8)
         return step, lax.rem(side + step // 4, 2) * 4 + lax.rem(col + lax.rem(step, 4), 4)
 
-    def near_step(index, carry):
-        lag = index // 8 + 1
-        step, dest = turn_target(lax.rem(index, 8))
+    def send_near(is_own, dest, lag):
         values = correlate(dest, lax.rem(dest + lag, 8))
         for part in range(2):
             place = (lag - 1) * 2 + part
             tiles[dest, place] = values[part].astype(jnp.bfloat16)
-            post(step == 0, dest, tiles.at[dest, place], near.at[channel, place], tile_sem.at[0], tile_sem.at[1], tile_sem.at[2])
-        return carry
-
-    lax.fori_loop(0, 24, near_step, 0)
-
-    def packed_step(index, carry):
-        step, dest = turn_target(index)
+            post(is_own, dest, tiles.at[dest, place], near.at[channel, place], tile_sem.at[0], tile_sem.at[1], tile_sem.at[2])
+
+    def send_packed(is_own, dest):
         real, imag = correlate(dest, dest)
         down = lax.broadcasted_iota(jnp.int32, (256, 256), 0)
         across = lax.broadcasted_iota(jnp.int32, (256, 256), 1)
         tiles[dest, 6] = jnp.where(down >= across, real, imag).astype(jnp.bfloat16)
-        post(step == 0, dest, tiles.at[dest, 6], near.at[channel, 6], tile_sem.at[0], tile_sem.at[1], tile_sem.at[2])
-        return carry
-
-    lax.fori_loop(0, 8, packed_step, 0)
+        post(is_own, dest, tiles.at[dest, 6], packed.at[channel], tile_sem.at[6], tile_sem.at[7], tile_sem.at[8])
+
+    def early_packed(index, carry):
+        dest = first * 4 + lax.rem(col + index + 1, 4)
+        send_packed(dest == blk, dest)
+        return carry
+
+    lax.fori_loop(0, 4, early_packed, 0)
+
+    def early_near(index, carry):
+        lag = lax.div(index, 4) + 1
+        dest_col = lax.rem(col + lax.rem(index, 4) + 1, 4)
+        dest = first * 4 + dest_col
+
+        @pl.when(dest_col + lag < 4)
+        def _():
+            send_near(dest == blk, dest, lag)
+
+        return carry
+
+    lax.fori_loop(0, 12, early_near, 0)
+
+    def take_second(group, carry):
+        wait_pieces(group, pl.ds(16, 16), 1, recv_sem)
+        take_half(group, second)
+        return carry
+
+    lax.fori_loop(WHOLE_GROUPS, GROUPS, take_second, 0)
+
+    def near_step(index, carry):
+        lag = lax.div(index, 8) + 1
+        step, dest = turn_target(lax.rem(index, 8))
+
+        @pl.when(jnp.logical_or(lax.div(dest, 4) != first, lax.rem(dest, 4) + lag >= 4))
+        def _():
+            send_near(step == 0, dest, lag)
+
+        return carry
+
+    def late_packed(index, carry):
+        dest = second * 4 + lax.rem(col + index + 1, 4)
+        send_packed(dest == blk, dest)
+        return carry
+
+    lax.fori_loop(0, 4, late_packed, 0)
+    lax.fori_loop(0, 24, near_step, 0)
 
     def far_step(index, carry):
         step = lax.rem(index + 1, 4)
@@ -339,15 +426,41 @@
 
     lax.fori_loop(0, 4, far_step, 0)
 
-    def finish(group, carry):
-        others = pl.ds(0, 127)
-        pltpu.make_async_copy(pieces.at[group, others], arrived.at[group, others], send_sem.at[group]).wait()
-        return carry
-
-    lax.fori_loop(0, GROUPS, finish, 0)
-    pltpu.make_async_copy(tiles.at[0], near.at[0], tile_sem.at[2]).wait()
+    def finish_whole(group, carry):
+        wait_pieces(group, slice(None), 0, send_sem)
+        return carry
+
+    def finish_halves(group, carry):
+        for half in range(2):
+            wait_pieces(group, pl.ds(half * 16, 16), half, send_sem)
+        return carry
+
+    lax.fori_loop(0, WHOLE_GROUPS, finish_whole, 0)
+    lax.fori_loop(WHOLE_GROUPS, GROUPS, finish_halves, 0)
+
+    pltpu.make_async_copy(tiles.at[0, 6], packed.at[0], tile_sem.at[8]).wait()
+    for sem in (6, 7):
+        pltpu.make_async_copy(packed.at[pl.ds(0, 7)], packed.at[pl.ds(0, 7)], tile_sem.at[sem]).wait()
+
+    def unpack(index, carry):
+        triangles = packed[index].astype(jnp.float32)
+        turned = triangles.T
+        down = lax.broadcasted_iota(jnp.int32, (256, 256), 0)
+        across = lax.broadcasted_iota(jnp.int32, (256, 256), 1)
+        unpacked[index, 0] = jnp.where(down >= across, triangles, turned).astype(jnp.bfloat16)
+        mirrored = jnp.where(down > across, -turned, 0.0)
+        unpacked[index, 1] = jnp.where(down < across, triangles, mirrored).astype(jnp.bfloat16)
+        return carry
+
+    lax.fori_loop(0, 8, unpack, 0)
+    unpacked_copy = pltpu.make_async_copy(unpacked, mirror, tile_sem.at[9])
+    unpacked_copy.start()
+    unpacked_copy.wait()
+
+    whole_parts = pl.ds(0, 6)
+    pltpu.make_async_copy(tiles.at[0, whole_parts], near.at[0, whole_parts], tile_sem.at[2]).wait()
     for sem in (0, 1):
-        pltpu.make_async_copy(tiles.at[pl.ds(0, 7)], near.at[pl.ds(0, 7)], tile_sem.at[sem]).wait()
+        pltpu.make_async_copy(tiles.at[pl.ds(0, 7), whole_parts], near.at[pl.ds(0, 7), whole_parts], tile_sem.at[sem]).wait()
     pltpu.make_async_copy(far_tiles.at[0], far.at[0], tile_sem.at[5]).wait()
     for sem in (3, 4):
         pltpu.make_async_copy(far_tiles.at[pl.ds(0, 3)], far.at[pl.ds(0, 3)], tile_sem.at[sem]).wait()
@@ -368,11 +481,12 @@
     return pl.pallas_call(
         correlator_kernel,
         out_shape=(
-            jax.ShapeDtypeStruct((8, 7, 256, 256), jnp.bfloat16),
+            jax.ShapeDtypeStruct((8, 6, 256, 256), jnp.bfloat16),
+            jax.ShapeDtypeStruct((8, 2, 256, 256), jnp.bfloat16),
             jax.ShapeDtypeStruct((4, 2, 256, 256), jnp.bfloat16),
         ),
         in_specs=[anywhere] + [pl.BlockSpec(memory_space=pltpu.VMEM)] * 3,
-        out_specs=(anywhere, anywhere),
+        out_specs=(anywhere, anywhere, anywhere),
         scratch_shapes=[pltpu.VMEM(voltages.shape, jnp.bfloat16)]
         + [
             pltpu.VMEM((COLS, 8, LANES), jnp.float32),
@@ -393,70 +507,58 @@
             pltpu.VMEM((8, 8, 256, LANES), jnp.bfloat16),
             pltpu.VMEM((8, 7, 256, 256), jnp.bfloat16),
             pltpu.VMEM((4, 2, 256, 256), jnp.bfloat16),
+            pltpu.VMEM((8, 256, 256), jnp.bfloat16),
+            pltpu.VMEM((8, 2, 256, 256), jnp.bfloat16),
             pltpu.SemaphoreType.DMA((GROUPS,)),
-            pltpu.SemaphoreType.DMA((GROUPS,)),
-            pltpu.SemaphoreType.DMA((GROUPS,)),
+            pltpu.SemaphoreType.DMA((2, GROUPS)),
+            pltpu.SemaphoreType.DMA((2, GROUPS)),
             pltpu.SemaphoreType.DMA((GROUPS,)),
             pltpu.SemaphoreType.DMA((2,)),
-            pltpu.SemaphoreType.DMA((6,)),
+            pltpu.SemaphoreType.DMA((10,)),
         ],
-        compiler_params=pltpu.CompilerParams(vmem_limit_bytes=42 * 2**20, collective_id=0, has_side_effects=True),
+        compiler_params=pltpu.CompilerParams(vmem_limit_bytes=44 * 2**20, collective_id=0, has_side_effects=True),
         cost_estimate=pl.CostEstimate(flops=10**10, bytes_accessed=16 * 2**20, transcendentals=0),
     )(voltages, order_table, pfb_taps, tables())
 
 
-def arrange_kernel(lag_table, near, far, visibility, far_visibility, unpacked, sems):
+def arrange_kernel(lag_table, near, mirror, far, visibility, far_visibility, sems):
     far_copy = pltpu.make_async_copy(far, far_visibility.at[:, 0], sems.at[0])
     far_copy.start()
     for slot in range(4):
         lag = lag_table[slot]
 
+        @pl.when(lag == 0)
+        def _(slot=slot):
+            for out in range(8):
+                pltpu.make_async_copy(mirror.at[out], visibility.at[out, 0, slot], sems.at[slot + 1]).start()
+
         @pl.when(lag > 0)
         def _(slot=slot, lag=lag):
-            pltpu.make_async_copy(near.at[:, pl.ds((lag - 1) * 2, 2)], visibility.at[:, 0, slot], sems.at[1]).start()
-
-    own_slot = 0
+            for out in range(8):
+                pltpu.make_async_copy(near.at[out, pl.ds((lag - 1) * 2, 2)], visibility.at[out, 0, slot], sems.at[slot + 1]).start()
+
     for slot in range(4):
-        own_slot = jnp.where(lag_table[slot] == 0, slot, own_slot)
-    down = lax.broadcasted_iota(jnp.int32, (256, 256), 0)
-    across = lax.broadcasted_iota(jnp.int32, (256, 256), 1)
-
-    def unpack(out, carry):
-        packed = near[out, 6].astype(jnp.float32)
-        turned = packed.T
-        unpacked[out, 0] = jnp.where(down >= across, packed, turned).astype(jnp.bfloat16)
-        mirrored = jnp.where(down > across, -turned, 0.0)
-        unpacked[out, 1] = jnp.where(down < across, packed, mirrored).astype(jnp.bfloat16)
-        pltpu.make_async_copy(unpacked.at[out], visibility.at[out, 0, own_slot], sems.at[2]).start()
-        return carry
-
-    lax.fori_loop(0, 8, unpack, 0)
+        pltpu.make_async_copy(mirror, visibility.at[:, 0, slot], sems.at[slot + 1]).wait()
     far_copy.wait()
-    for slot in range(4):
-        @pl.when(lag_table[slot] > 0)
-        def _(slot=slot):
-            pltpu.make_async_copy(near.at[:, pl.ds(0, 2)], visibility.at[:, 0, slot], sems.at[1]).wait()
-
-    pltpu.make_async_copy(unpacked, visibility.at[:, 0, 0], sems.at[2]).wait()
-
-
-def arrange(near, far, lag_table):
+
+
+def arrange(near, mirror, far, lag_table):
     return pl.pallas_call(
         arrange_kernel,
         out_shape=(
             jax.ShapeDtypeStruct((8, 1, 4, 2, 256, 256), jnp.bfloat16),
             jax.ShapeDtypeStruct((4, 1, 2, 256, 256), jnp.bfloat16),
         ),
-        in_specs=[pl.BlockSpec(memory_space=pltpu.SMEM), pl.BlockSpec(memory_space=pltpu.VMEM), pl.BlockSpec(memory_space=pltpu.VMEM)],
+        in_specs=[pl.BlockSpec(memory_space=pltpu.SMEM)] + [pl.BlockSpec(memory_space=pltpu.VMEM)] * 3,
         out_specs=(pl.BlockSpec(memory_space=pl.ANY), pl.BlockSpec(memory_space=pl.ANY)),
-        scratch_shapes=[pltpu.VMEM((8, 2, 256, 256), jnp.bfloat16), pltpu.SemaphoreType.DMA((3,))],
-        compiler_params=pltpu.CompilerParams(vmem_limit_bytes=16 * 2**20),
-    )(lag_table, near, far)
+        scratch_shapes=[pltpu.SemaphoreType.DMA((5,))],
+        compiler_params=pltpu.CompilerParams(vmem_limit_bytes=2**20),
+    )(lag_table, near, mirror, far)
 
 
 def per_device(voltages, pfb_taps, order_table, lag_table):
-    near, far = make_tiles(voltages, pfb_taps, order_table)
-    return arrange(near, far, lag_table)
+    near, mirror, far = make_tiles(voltages, pfb_taps, order_table)
+    return arrange(near, mirror, far, lag_table)
 
 
 def solution(mesh):

time: 165 us -> 160 us (0.970)
  Pallas kernels: 162 us -> 157 us
    pallas_call x1, Pallas kernels: 158 us -> 152 us  [make_tiles(): pl.pallas_call(correlator_kernel, out_shape=(jax.ShapeDtypeStruct((8, 6,...]
where the time goes in v5:
time: 160 us
  Pallas kernels  157 us (98%)
  local copies, waits for them, and re-layouts  2.59 us (2%)
    pallas_call x1, Pallas kernels, make_tiles(): pl.pallas_call(correlator_kernel, out_shape=(jax.ShapeDtypeStruct((8, 6,...  152 us
    pallas_call x1, Pallas kernels, arrange(): pl.pallas_call(arrange_kernel, out_shape=(jax.ShapeDtypeStruct((8, 1, 4,...  4.15 us

profile of v5, /device:TPU:1, one launch (start us, length us, event | category | flops | bytes accessed | tf_op | source)
XLA Modules:
  0.0 159.9 jit_solution(4934677559395784771)
XLA Ops:
  0.6 0.0 copy-start
  0.6 0.0 copy-start.1
  0.7 0.9 copy-done.1
  1.6 0.0 copy-start.2
  1.6 0.7 copy-done.2
  2.3 0.0 copy-start.3
  2.3 1.0 copy-done.3
  3.2 152.5 %shard_map.68 = (bf16[8,6,256,256]{3,2,1,0:T(8,128)(2,1)S(1)}, bf16[8,2,256,256]{3,2,1,0:T(8,128)(2,1)S(1)}, bf16[4,2,256,256]{3,2,1,0:T(8,128)(2,1)S(1)}) custom-call(bf16[2,16,126976]{2,1,0:T(8,128)(2,1)} %volt_far.1, s32[1,256]{1,0:T(1,128)S(1)} %copy-done.2, f32[16,4096]{1,0:T(8,128)S(1)} %copy-done.1, f32[576,128]{1,0:T(8,128)S(1)} %copy-done.3), custom_call_target="tpu_custom_call" | custom-call | flops 10000000000 | bytes 16777216 | tf_op jit(solution)/shard_map/pallas_call | solution.py:481
  155.7 0.0 copy-done
  155.7 4.2 %shard_map.69 = (bf16[8,1,4,2,256,256]{5,4,3,2,1,0:T(8,128)(2,1)}, bf16[4,1,2,256,256]{4,3,2,1,0:T(8,128)(2,1)}) custom-call(s32[4]{0:T(128)S(1)} %copy-done, bf16[8,6,256,256]{3,2,1,0:T(8,128)(2,1)S(1)} %get-tuple-element.5.near, bf16[8,2,256,256]{3,2,1,0:T(8,128)(2,1)S(1)} %get-tuple-element.6.mirror, bf16[4,2,256,256]{3,2,1,0:T(8,128)(2,1)S(1)} %get-tuple-element.7.far), custom_call_target="tpu_custom_call" | custom-call | tf_op jit(solution)/shard_map/pallas_call | solution.py:546
Async XLA Ops:
  0.6 155.1 %copy-start = (s32[4]{0:T(128)S(1)}, s32[4]{0:T(128)}, u32[]{:S(2)}) copy-start(s32[4]{0:T(128)} %lag_table.1) | copy-start | bytes 52
  0.6 1.0 copy-start.1
  1.6 0.7 copy-start.2
  2.3 1.0 copy-start.3

commit v6 on v5

--- a/solution.py
+++ b/solution.py
@@ -85,8 +85,20 @@
     return (layer * 4 + (row // 2) * 2 + core, lax.rem(row, 2) * 4 + col)
 
 
+def unit_circle(steps, count):
+    centered = jnp.where(steps > count // 2, steps - count, steps).astype(jnp.float32)
+    angle = centered * (2 * math.pi / count)
+    square = angle * angle
+    cos = jnp.zeros_like(angle)
+    sin = jnp.zeros_like(angle)
+    for order in range(9, -1, -1):
+        cos = cos * square + (-1) ** order / math.factorial(2 * order)
+        sin = sin * square + (-1) ** order / math.factorial(2 * order + 1)
+    return cos, sin * angle
+
+
 def correlator_kernel(
-    volt_far, order_row, taps, numbers,
+    volt_far, order_row, taps,
     near, mirror, far,
     volt, turn_cos, turn_sin, dft_high, dft_low, spread,
     filt, z_real, z_imag, wide, pieces, arrived, own_order, orders, chosen, natural, rows, tiles, far_tiles, packed, unpacked,
@@ -135,12 +147,19 @@
 
     visit_others(greet)
     own_order[...] = jnp.broadcast_to(order_row[...], (8, 256))
+    fine = lax.broadcasted_iota(jnp.int32, (COLS, LANES), 0) * lax.broadcasted_iota(jnp.int32, (COLS, LANES), 1)
+    fine_cos, fine_sin = unit_circle(fine, CH)
     for index in range(COLS):
-        turn_cos[index] = jnp.broadcast_to(numbers[index:index + 1, :], (8, LANES))
-        turn_sin[index] = jnp.broadcast_to(numbers[COLS + index:COLS + index + 1, :], (8, LANES))
-    dft = jnp.concatenate([numbers[2 * COLS:2 * COLS + 256, :], numbers[2 * COLS + 256:2 * COLS + 512, :]], axis=1)
-    dft_high[...] = dft.astype(jnp.bfloat16)
-    dft_low[...] = (dft - dft.astype(jnp.bfloat16).astype(jnp.float32)).astype(jnp.bfloat16)
+        turn_cos[index] = jnp.broadcast_to(fine_cos[index:index + 1, :] * (1.0 / 64), (8, LANES))
+        turn_sin[index] = jnp.broadcast_to(fine_sin[index:index + 1, :] * (-1.0 / 64), (8, LANES))
+    coarse = lax.broadcasted_iota(jnp.int32, (LANES, LANES), 0) * lax.broadcasted_iota(jnp.int32, (LANES, LANES), 1)
+    dft_cos, dft_sin = unit_circle(jnp.bitwise_and(coarse, LANES - 1), LANES)
+    for part, tables in enumerate(((dft_cos, dft_sin), (-dft_sin, dft_cos))):
+        for half, table in enumerate(tables):
+            place = (slice(part * LANES, part * LANES + LANES), slice(half * LANES, half * LANES + LANES))
+            high = table.astype(jnp.bfloat16)
+            dft_high[place] = high
+            dft_low[place] = (table - high.astype(jnp.float32)).astype(jnp.bfloat16)
     sorted_row = lax.broadcasted_iota(jnp.int32, (256, 256), 0)
     came_row = lax.broadcasted_iota(jnp.int32, (256, 256), 1)
     wanted = jnp.bitwise_and(sorted_row, 30) * 8 + lax.shift_right_logical(sorted_row, 5) * 2 + jnp.bitwise_and(sorted_row, 1)
@@ -353,7 +372,7 @@
             ).start()
 
     def turn_target(turn):
-        step = lax.rem(turn * 3 + 1, 8)
+        step = lax.rem(turn * 5 + 1, 8)
         return step, lax.rem(side + step // 4, 2) * 4 + lax.rem(col + lax.rem(step, 4), 4)
 
     def send_near(is_own, dest, lag):
@@ -388,7 +407,7 @@
 
         return carry
 
-    lax.fori_loop(0, 12, early_near, 0)
+    lax.fori_loop(0, 4, early_near, 0)
 
     def take_second(group, carry):
         wait_pieces(group, pl.ds(16, 16), 1, recv_sem)
@@ -401,7 +420,7 @@
         lag = lax.div(index, 8) + 1
         step, dest = turn_target(lax.rem(index, 8))
 
-        @pl.when(jnp.logical_or(lax.div(dest, 4) != first, lax.rem(dest, 4) + lag >= 4))
+        @pl.when(jnp.logical_or(lax.div(dest, 4) != first, jnp.logical_or(lag > 1, lax.rem(dest, 4) + lag >= 4)))
         def _():
             send_near(step == 0, dest, lag)
 
@@ -412,8 +431,9 @@
         send_packed(dest == blk, dest)
         return carry
 
+    lax.fori_loop(0, 16, near_step, 0)
     lax.fori_loop(0, 4, late_packed, 0)
-    lax.fori_loop(0, 24, near_step, 0)
+    lax.fori_loop(16, 24, near_step, 0)
 
     def far_step(index, carry):
         step = lax.rem(index + 1, 4)
@@ -464,16 +484,6 @@
     pltpu.make_async_copy(far_tiles.at[0], far.at[0], tile_sem.at[5]).wait()
     for sem in (3, 4):
         pltpu.make_async_copy(far_tiles.at[pl.ds(0, 3)], far.at[pl.ds(0, 3)], tile_sem.at[sem]).wait()
-
-
-def tables():
-    rows = np.arange(COLS)[:, None] * np.arange(LANES)[None, :]
-    angles = -2.0 * np.pi * rows / CH
-    steps = np.arange(LANES)
-    turn = -2.0 * np.pi * (steps[:, None] * steps[None, :] % LANES) / LANES
-    dft = np.block([[np.cos(turn), -np.sin(turn)], [np.sin(turn), np.cos(turn)]])
-    parts = [np.cos(angles) / 64, np.sin(angles) / 64, dft[:, :LANES], dft[:, LANES:]]
-    return jnp.asarray(np.concatenate(parts, axis=0), jnp.float32)
 
 
 def make_tiles(voltages, pfb_taps, order_table):
@@ -485,7 +495,7 @@
             jax.ShapeDtypeStruct((8, 2, 256, 256), jnp.bfloat16),
             jax.ShapeDtypeStruct((4, 2, 256, 256), jnp.bfloat16),
         ),
-        in_specs=[anywhere] + [pl.BlockSpec(memory_space=pltpu.VMEM)] * 3,
+        in_specs=[anywhere] + [pl.BlockSpec(memory_space=pltpu.VMEM)] * 2,
         out_specs=(anywhere, anywhere, anywhere),
         scratch_shapes=[pltpu.VMEM(voltages.shape, jnp.bfloat16)]
         + [
@@ -518,7 +528,7 @@
         ],
         compiler_params=pltpu.CompilerParams(vmem_limit_bytes=44 * 2**20, collective_id=0, has_side_effects=True),
         cost_estimate=pl.CostEstimate(flops=10**10, bytes_accessed=16 * 2**20, transcendentals=0),
-    )(voltages, order_table, pfb_taps, tables())
+    )(voltages, order_table, pfb_taps)
 
 
 def arrange_kernel(lag_table, near, mirror, far, visibility, far_visibility, sems):

time: 160 us -> 157 us (0.981)
  Pallas kernels: 157 us -> 155 us
    pallas_call x1, Pallas kernels: 152 us -> 151 us  [make_tiles(): pl.pallas_call(correlator_kernel, out_shape=(jax.ShapeDtypeStruct((8, 6,...]
where the time goes in v6:
time: 157 us
  Pallas kernels  155 us (99%)
  local copies, waits for them, and re-layouts  1.63 us (1%)
    pallas_call x1, Pallas kernels, make_tiles(): pl.pallas_call(correlator_kernel, out_shape=(jax.ShapeDtypeStruct((8, 6,...  151 us
    pallas_call x1, Pallas kernels, arrange(): pl.pallas_call(arrange_kernel, out_shape=(jax.ShapeDtypeStruct((8, 1, 4,...  4.15 us

profile of v6, /device:TPU:1, one launch (start us, length us, event | category | flops | bytes accessed | tf_op | source)
XLA Modules:
  0.0 157.0 jit_solution(3704365850696477201)
XLA Ops:
  0.6 0.0 copy-start
  0.6 0.0 copy-start.1
  0.7 0.9 copy-done.1
  1.6 0.0 copy-start.2
  1.6 0.7 copy-done.2
  2.3 150.6 %shard_map.59 = (bf16[8,6,256,256]{3,2,1,0:T(8,128)(2,1)S(1)}, bf16[8,2,256,256]{3,2,1,0:T(8,128)(2,1)S(1)}, bf16[4,2,256,256]{3,2,1,0:T(8,128)(2,1)S(1)}) custom-call(bf16[2,16,126976]{2,1,0:T(8,128)(2,1)} %volt_far.1, s32[1,256]{1,0:T(1,128)S(1)} %copy-done.2, f32[16,4096]{1,0:T(8,128)S(1)} %copy-done.1), custom_call_target="tpu_custom_call" | custom-call | flops 10000000000 | bytes 16777216 | tf_op jit(solution)/shard_map/pallas_call | solution.py:491
  152.9 0.0 copy-done
  152.9 4.2 %shard_map.60 = (bf16[8,1,4,2,256,256]{5,4,3,2,1,0:T(8,128)(2,1)}, bf16[4,1,2,256,256]{4,3,2,1,0:T(8,128)(2,1)}) custom-call(s32[4]{0:T(128)S(1)} %copy-done, bf16[8,6,256,256]{3,2,1,0:T(8,128)(2,1)S(1)} %get-tuple-element.5.near, bf16[8,2,256,256]{3,2,1,0:T(8,128)(2,1)S(1)} %get-tuple-element.6.mirror, bf16[4,2,256,256]{3,2,1,0:T(8,128)(2,1)S(1)} %get-tuple-element.7.far), custom_call_target="tpu_custom_call" | custom-call | tf_op jit(solution)/shard_map/pallas_call | solution.py:556
Async XLA Ops:
  0.6 152.2 %copy-start = (s32[4]{0:T(128)S(1)}, s32[4]{0:T(128)}, u32[]{:S(2)}) copy-start(s32[4]{0:T(128)} %lag_table.1) | copy-start | bytes 52
  0.6 1.0 copy-start.1
  1.6 0.7 copy-start.2

commit v7 on v6

--- a/solution.py
+++ b/solution.py
@@ -505,9 +505,9 @@
             pltpu.VMEM((256, 256), jnp.bfloat16),
             pltpu.VMEM((256, 256), jnp.bfloat16),
             pltpu.VMEM((2, GROUP, COLS, 16, LANES), jnp.float32),
-            pltpu.VMEM((8 * Z_STRIDE, LANES), jnp.float32),
-            pltpu.VMEM((8 * Z_STRIDE, LANES), jnp.float32),
-            pltpu.VMEM((128 * WIDE_STRIDE, LANES), jnp.float32),
+            pltpu.VMEM((9 * Z_STRIDE, LANES), jnp.float32),
+            pltpu.VMEM((9 * Z_STRIDE, LANES), jnp.float32),
+            pltpu.VMEM((129 * WIDE_STRIDE, LANES), jnp.float32),
             pltpu.VMEM((GROUPS, 128, 32, LANES), jnp.bfloat16),
             pltpu.VMEM((GROUPS, 128, 32, LANES), jnp.bfloat16),
             pltpu.VMEM((8, 256), jnp.int32),

time: 157 us -> 157 us (level)
  no operation moved by 1% of the time
where the time goes in v7:
time: 157 us
  Pallas kernels  155 us (99%)
  local copies, waits for them, and re-layouts  1.63 us (1%)
    pallas_call x1, Pallas kernels, make_tiles(): pl.pallas_call(correlator_kernel, out_shape=(jax.ShapeDtypeStruct((8, 6,...  151 us
    pallas_call x1, Pallas kernels, arrange(): pl.pallas_call(arrange_kernel, out_shape=(jax.ShapeDtypeStruct((8, 1, 4,...  4.15 us

profile of v7, /device:TPU:1, one launch (start us, length us, event | category | flops | bytes accessed | tf_op | source)
XLA Modules:
  0.0 157.0 jit_solution(3991411299546135197)
XLA Ops:
  0.6 0.0 copy-start
  0.6 0.0 copy-start.1
  0.7 0.9 copy-done.1
  1.6 0.0 copy-start.2
  1.6 0.7 copy-done.2
  2.3 150.5 %shard_map.59 = (bf16[8,6,256,256]{3,2,1,0:T(8,128)(2,1)S(1)}, bf16[8,2,256,256]{3,2,1,0:T(8,128)(2,1)S(1)}, bf16[4,2,256,256]{3,2,1,0:T(8,128)(2,1)S(1)}) custom-call(bf16[2,16,126976]{2,1,0:T(8,128)(2,1)} %volt_far.1, s32[1,256]{1,0:T(1,128)S(1)} %copy-done.2, f32[16,4096]{1,0:T(8,128)S(1)} %copy-done.1), custom_call_target="tpu_custom_call" | custom-call | flops 10000000000 | bytes 16777216 | tf_op jit(solution)/shard_map/pallas_call | solution.py:491
  152.8 0.0 copy-done
  152.8 4.2 %shard_map.60 = (bf16[8,1,4,2,256,256]{5,4,3,2,1,0:T(8,128)(2,1)}, bf16[4,1,2,256,256]{4,3,2,1,0:T(8,128)(2,1)}) custom-call(s32[4]{0:T(128)S(1)} %copy-done, bf16[8,6,256,256]{3,2,1,0:T(8,128)(2,1)S(1)} %get-tuple-element.5.near, bf16[8,2,256,256]{3,2,1,0:T(8,128)(2,1)S(1)} %get-tuple-element.6.mirror, bf16[4,2,256,256]{3,2,1,0:T(8,128)(2,1)S(1)} %get-tuple-element.7.far), custom_call_target="tpu_custom_call" | custom-call | tf_op jit(solution)/shard_map/pallas_call | solution.py:556
Async XLA Ops:
  0.6 152.2 %copy-start = (s32[4]{0:T(128)S(1)}, s32[4]{0:T(128)}, u32[]{:S(2)}) copy-start(s32[4]{0:T(128)} %lag_table.1) | copy-start | bytes 52
  0.6 1.0 copy-start.1
  1.6 0.7 copy-start.2
